TPU v7x, 256 devices: a whole 4x4x8 slice. The times are simulated.
256 devices in a mesh: seg: 64 (over x, z, core), head: 4 (over y).
Axes of the slice: x: 4, y: 4, z: 8, core: 2. Of those that a mesh axis runs over, the one named last changes fastest.
Arguments:
- tokens: bfloat16 [65536, 1024], P('seg'), may hold values from -50 to 50
- norm_gain: bfloat16 [1024], replicated, may hold values from 0.099609375 to 1.8984375
- qkv_weight: bfloat16 [3, 1024, 1024], P(None, None, 'head'), may hold values from -1.5 to 1.5
- out_weight: bfloat16 [1024, 1024], replicated, may hold values from -0.1875 to 0.1875
- offsets: int32 [16, 2], P('head'), may hold values from 0 to 31, as said below
Outputs:
- projected: bfloat16 [65536, 1024], P('seg', 'head')
Inputs may be any that keep to these rules, and one draw needn't show every extreme that they name: offsets[h, 0] is below 4 and offsets[h, 1] below 32.
All inputs are finite; a program needn't handle non-finite values.
Results may differ from a plain program's by a relative error of at most 0.012.
The roundings to bfloat16 on the way count: a program that leaves them out, or rounds other values in their place, can miss the bound.
Values may be sent and summed in bfloat16 or wider, within the bound.
No kernel may reach another device: no remote copies, remote signals or barrier semaphores. Data moves between devices by JAX's collectives and lax.ppermute only.
A program may use at most 128 MiB of HBM per device.

v0:
```python
import jax
import jax.numpy as jnp
from jax import lax
from jax.sharding import PartitionSpec as P

HEAD_DIM = 64
MID_RATE = 4


EPS = 1e-06
NEG = -1e30


def from_partner(shard, axis, stride):
    return lax.ppermute(shard, axis, [(i, i ^ 1 << stride) for i in range(lax.axis_size(axis))])


def attend_head(queries, key_rows, value_rows):
    scores = jnp.dot(queries, key_rows.T, preferred_element_type=jnp.float32) * HEAD_DIM ** (-0.5)
    row_peak = jnp.max(scores, axis=1, keepdims=True)
    weights = jnp.exp(scores - row_peak)
    row_total = jnp.sum(weights, axis=1, keepdims=True)
    blended = (
        jnp.dot(weights.astype(jnp.bfloat16), value_rows, preferred_element_type=jnp.float32)
        / row_total
    )
    return (blended, row_peak[:, 0] + jnp.log(row_total[:, 0]))


def head_items(items):
    return attend_head(items[0], items[1], items[2])


def attend_heads(queries, packed):
    head_count = queries.shape[1]
    grouped = packed.reshape(packed.shape[0], head_count, 2, HEAD_DIM)
    blended, log_total = lax.map(
        head_items,
        (
            jnp.transpose(queries, (1, 0, 2)),
            jnp.transpose(grouped[:, :, 0], (1, 0, 2)),
            jnp.transpose(grouped[:, :, 1], (1, 0, 2)),
        ),
    )
    return (jnp.transpose(blended, (1, 0, 2)), jnp.transpose(log_total))


def strided(values_in, dilation, offset):
    row_count, head_count, features = values_in.shape
    chosen = (jnp.arange(dilation, dtype=jnp.int32)[:, None] == offset[None, :]).astype(
        values_in.dtype
    )
    grouped = values_in.reshape(row_count // dilation, dilation, head_count, features)
    return jnp.sum(grouped * chosen[None, :, :, None], axis=1)


def spread_back(blended, log_total, dilation, offset):
    row_count, head_count, features = blended.shape
    chosen = jnp.arange(dilation, dtype=jnp.int32)[:, None] == offset[None, :]
    full = jnp.where(chosen[None, :, :, None], blended[:, None], 0.0).reshape(
        row_count * dilation, head_count, features
    )
    full_log = jnp.where(chosen[None], log_total[:, None], NEG).reshape(
        row_count * dilation, head_count
    )
    return (full, full_log)


def ordered(mine, theirs, section_bit):
    upper = lax.axis_index("seg") // 2**section_bit % 2 == 1
    return jnp.concatenate([jnp.where(upper, theirs, mine), jnp.where(upper, mine, theirs)], axis=0)


def shards(tokens, norm_gain, qkv_weight, out_weight, offsets):
    row_count = tokens.shape[0]
    head_count = qkv_weight.shape[2] // HEAD_DIM
    far_rate = lax.axis_size("seg") // 2
    widened = tokens.astype(jnp.float32)
    mean_square = jnp.mean(widened * widened, axis=1, keepdims=True)
    normed = (widened * lax.rsqrt(mean_square + EPS) * norm_gain.astype(jnp.float32)).astype(
        jnp.bfloat16
    )
    queries = (
        jnp.dot(normed, qkv_weight[0], preferred_element_type=jnp.float32)
        .astype(jnp.bfloat16)
        .reshape(row_count, head_count, HEAD_DIM)
    )
    key_rows = (
        jnp.dot(normed, qkv_weight[1], preferred_element_type=jnp.float32)
        .astype(jnp.bfloat16)
        .reshape(row_count, head_count, 1, HEAD_DIM)
    )
    value_rows = (
        jnp.dot(normed, qkv_weight[2], preferred_element_type=jnp.float32)
        .astype(jnp.bfloat16)
        .reshape(row_count, head_count, 1, HEAD_DIM)
    )
    packed = jnp.concatenate([key_rows, value_rows], axis=2).reshape(
        row_count, head_count, 2 * HEAD_DIM
    )
    middle_offset = offsets[:, 0]
    far_offset = offsets[:, 1]
    packed_width = head_count * 2 * HEAD_DIM
    near_local = packed.reshape(row_count, packed_width)
    middle_local = strided(packed, MID_RATE, middle_offset).reshape(
        row_count // MID_RATE, packed_width
    )
    far_local = strided(packed, far_rate, far_offset).reshape(row_count // far_rate, packed_width)
    middle_bits = (2 * MID_RATE).bit_length() - 1
    near_keys = ordered(near_local, from_partner(near_local, "seg", 0), 0)
    middle_keys = middle_local
    for section_bit in range(middle_bits):
        middle_keys = ordered(
            middle_keys, from_partner(middle_keys, "seg", section_bit), section_bit
        )
    far_keys = lax.all_gather(far_local, "seg", axis=0, tiled=True)
    near_out, near_log = attend_heads(queries, near_keys)
    middle_blend, middle_total = attend_heads(
        strided(queries, MID_RATE, middle_offset), middle_keys
    )
    middle_out, middle_log = spread_back(middle_blend, middle_total, MID_RATE, middle_offset)
    far_blend, far_total = attend_heads(strided(queries, far_rate, far_offset), far_keys)
    far_out, far_log = spread_back(far_blend, far_total, far_rate, far_offset)
    row_peak = jnp.maximum(jnp.maximum(near_log, middle_log), far_log)
    near_weight = jnp.exp(near_log - row_peak)[:, :, None]
    middle_weight = jnp.exp(middle_log - row_peak)[:, :, None]
    far_weight = jnp.exp(far_log - row_peak)[:, :, None]
    combined = (near_weight * near_out + middle_weight * middle_out + far_weight * far_out) / (
        near_weight + middle_weight + far_weight
    )
    attention = combined.astype(jnp.bfloat16).reshape(row_count, head_count * HEAD_DIM)
    column_count = out_weight.shape[1] // lax.axis_size("head")
    own_columns = lax.dynamic_slice_in_dim(
        out_weight, lax.axis_index("head") * column_count, column_count, 1
    )
    summed = jnp.dot(
        lax.all_gather(attention, "head", axis=1, tiled=True),
        own_columns,
        preferred_element_type=jnp.float32,
    )
    return summed.astype(jnp.bfloat16)


def solution(mesh):
    placed = (P("seg", None), P(), P(None, None, "head"), P(), P("head", None))
    return jax.shard_map(
        shards, mesh=mesh, in_specs=placed, out_specs=P("seg", "head"), check_vma=False
    )
```

profile of v0, /device:TPU:1, one launch (start us, length us, event | category | flops | bytes accessed | tf_op | source)
XLA Modules:
  0.0 217.3 jit_solution(7214449474174543522)
XLA Ops:
  13.1 3.3 %collective-permute-start = (bf16[1024,512]{0,1:T(8,128)(2,1)S(1)}, bf16[1024,512]{0,1:T(8,128)(2,1)}, u32[]{:S(2)}, u32[]{:S(2)}) collective-permute-start(bf16[1024,512]{0,1:T(8,128)(2,1)S(1)} %bitcast.203), channel_id=1, source_target_pairs={{0,4},{4,0},{8,12},{12,8},{16,20},{20,16},{24,28},{28,24},{32,36},... | collective-permute-start | bytes 3145736 | tf_op jit(solution)/shard_map/ppermute | solution.py:15
  16.4 3.9 %copy.105 = bf16[1024,4,2,64]{3,2,1,0:T(2,128)(2,1)} copy(bf16[1024,4,2,64]{0,3,2,1:T(8,128)(2,1)S(1)} %pad_maximum_fusion.2) | data formatting | bytes 2097152 | tf_op jit(solution)/shard_map/concatenate | solution.py:98
  20.3 5.1 %reshape_reshape.17 = bf16[256,4,4,128]{3,2,1,0:T(4,128)(2,1)} reshape(bf16[1024,4,2,64]{3,2,1,0:T(2,128)(2,1)} %copy.105) | data formatting | bytes 2097152 | tf_op jit(solution)/shard_map/reshape;reshape | solution.py:53
  25.4 2.9 %multiply_reduce_fusion.3 = bf16[256,4,128]{2,1,0:T(4,128)(2,1)} fusion(bf16[256,4,4,128]{3,2,1,0:T(4,128)(2,1)} %reshape_reshape.17, bf16[4,4]{1,0:T(4,128)(2,1)S(1)} %get-tuple-element.263), kind=kLoop, calls=%fused_computation.81 | loop fusion | flops 917504 | bytes 1310752 | tf_op jit(solution)/shard_map/reduce_sum | solution.py:54
  29.5 3.8 %copy.114 = bf16[1024,4,2,64]{3,2,0,1:T(2,128)(2,1)} copy(bf16[1024,4,2,64]{0,3,2,1:T(8,128)(2,1)S(1)} %pad_maximum_fusion.2) | data formatting | bytes 2097152 | tf_op jit(solution)/shard_map/concatenate | solution.py:98
  33.3 4.7 %reshape_reshape.19 = bf16[32,32,4,128]{3,1,0,2:T(8,128)(2,1)} reshape(bf16[1024,4,2,64]{3,2,0,1:T(2,128)(2,1)} %copy.114) | data formatting | bytes 2097152 | tf_op jit(solution)/shard_map/reshape;reshape | solution.py:53
  43.4 2.8 %convolution_convert_fusion.3 = bf16[1024,256]{0,1:T(8,128)(2,1)} fusion(bf16[3,1024,256]{2,1,0:T(8,128)(2,1)} %param.13, bf16[1024,1024]{1,0:T(8,128)(2,1)S(1)} %copy-done.11, f32[1024]{0:T(1024)S(1)} %convert_element_type.58, f32[1024]{0:T(1024)S(1)} %add_rsqrt_fusion), kind=kOutput, calls=%fused_computation.70 | convolution fusion | flops 541327360 | bytes 3153920 | tf_op jit(solution)/shard_map/dot_general | solution.py:84
  48.3 2.8 %reshape_reshape.16 = bf16[256,4,4,64]{3,2,1,0:T(4,128)(2,1)} reshape(bf16[1024,256]{1,0:T(8,128)(2,1)} %copy.104) | data formatting | bytes 1048576 | tf_op jit(solution)/shard_map/reshape;reshape | solution.py:53
  51.0 2.8 %reshape_reshape.18 = bf16[32,32,4,64]{3,2,1,0:T(4,128)(2,1)} reshape(bf16[1024,256]{1,0:T(8,128)(2,1)} %copy.104) | data formatting | bytes 1048576 | tf_op jit(solution)/shard_map/reshape;reshape | solution.py:53
  64.8 2.9 %collective-permute-start.3 = (bf16[1024,512]{0,1:T(8,128)(2,1)}, bf16[1024,512]{0,1:T(8,128)(2,1)}, u32[]{:S(2)}, u32[]{:S(2)}) collective-permute-start(bf16[1024,512]{0,1:T(8,128)(2,1)} %pad_maximum_fusion.3), channel_id=1, source_target_pairs={{0,16},{4,20},{8,24},{12,28},{16,0},{20,4},{24,8},{28,12},{32,48},... | collective-permute-start | bytes 3145736 | tf_op jit(solution)/shard_map/ppermute | solution.py:15
  70.4 45.0 %while.36 = (s32[]{:T(128)}, f32[4,1024,64]{1,2,0:T(8,128)}, f32[4,1024]{1,0:T(4,128)S(1)}, bf16[4,1024,64]{2,1,0:T(8,128)(2,1)}, bf16[4,2048,64]{1,2,0:T(8,128)...) while((s32[]{:T(128)}, f32[4,1024,64]{1,2,0:T(8,128)}, f32[4,1024]{1,0:T(4,128)S(1)}, ...), condition=%wide.region_4.5_spmd, body=%wide.region_1.4_spmd.sunk | while | flops 553712640 | bytes 59811956 | solution.py:37
  76.0 5.7 %fusion.96 = f32[4,1024,64]{1,2,0:T(8,128)} fusion(f32[4,1024,64]{1,2,0:T(8,128)} %get-tuple-element.422, s32[]{:T(128)} %get-tuple-element.421, f32[1024,2048]{1,0:T(8,128)} %copy-done.1, f32[1024]{0:T(1024)S(1)} %get-tuple-element.372, bf16[4,2048,64]{1,2,0:T(8,128)(2,1)} %get-tuple-element.434, f32[1024]{0:T(1024)S(1)} %fusion.95), kind=kOutput, calls=%fused_computation.7.clone.1 | convolution fusion | flops 274792448 | bytes 8922112 | tf_op jit(solution)/shard_map/while/body/eval_jaxpr/dot_general | solution.py:24
  87.2 5.7 %fusion.96 = f32[4,1024,64]{1,2,0:T(8,128)} fusion(f32[4,1024,64]{1,2,0:T(8,128)} %get-tuple-element.422, s32[]{:T(128)} %get-tuple-element.421, f32[1024,2048]{1,0:T(8,128)} %copy-done.1, f32[1024]{0:T(1024)S(1)} %get-tuple-element.372, bf16[4,2048,64]{1,2,0:T(8,128)(2,1)} %get-tuple-element.434, f32[1024]{0:T(1024)S(1)} %fusion.95), kind=kOutput, calls=%fused_computation.7.clone.1 | convolution fusion | flops 274792448 | bytes 8922112 | tf_op jit(solution)/shard_map/while/body/eval_jaxpr/dot_general | solution.py:24
  98.5 5.7 %fusion.96 = f32[4,1024,64]{1,2,0:T(8,128)} fusion(f32[4,1024,64]{1,2,0:T(8,128)} %get-tuple-element.422, s32[]{:T(128)} %get-tuple-element.421, f32[1024,2048]{1,0:T(8,128)} %copy-done.1, f32[1024]{0:T(1024)S(1)} %get-tuple-element.372, bf16[4,2048,64]{1,2,0:T(8,128)(2,1)} %get-tuple-element.434, f32[1024]{0:T(1024)S(1)} %fusion.95), kind=kOutput, calls=%fused_computation.7.clone.1 | convolution fusion | flops 274792448 | bytes 8922112 | tf_op jit(solution)/shard_map/while/body/eval_jaxpr/dot_general | solution.py:24
  109.7 5.7 %fusion.96 = f32[4,1024,64]{1,2,0:T(8,128)} fusion(f32[4,1024,64]{1,2,0:T(8,128)} %get-tuple-element.422, s32[]{:T(128)} %get-tuple-element.421, f32[1024,2048]{1,0:T(8,128)} %copy-done.1, f32[1024]{0:T(1024)S(1)} %get-tuple-element.372, bf16[4,2048,64]{1,2,0:T(8,128)(2,1)} %get-tuple-element.434, f32[1024]{0:T(1024)S(1)} %fusion.95), kind=kOutput, calls=%fused_computation.7.clone.1 | convolution fusion | flops 274792448 | bytes 8922112 | tf_op jit(solution)/shard_map/while/body/eval_jaxpr/dot_general | solution.py:24
  115.5 3.3 %copy.120 = f32[4,1024,64]{2,1,0:T(8,128)} copy(f32[4,1024,64]{1,2,0:T(8,128)} %get-tuple-element.107) | data formatting | bytes 2097152 | tf_op jit(solution)/shard_map/while | solution.py:37
  121.8 21.6 %while.37 = (s32[]{:T(128)}, f32[4,256,64]{1,2,0:T(8,128)S(1)}, f32[4,256]{1,0:T(4,128)S(1)}, bf16[4,256,64]{2,1,0:T(8,128)(2,1)}, bf16[4,2048,64]{1,2,0:T(8,128...) while((s32[]{:T(128)}, f32[4,256,64]{1,2,0:T(8,128)S(1)}, f32[4,256]{1,0:T(4,128)S(1)}, ...), condition=%wide.region_10.11_spmd, body=%wide.region_7.10_spmd.sunk | while | flops 137379584 | bytes 15347829 | solution.py:37
  144.9 7.8 %all-gather.3.cloned.1.call-done = bf16[2048,512]{1,0:T(8,128)(2,1)} async-done(((bf16[32,512]{1,0:T(8,128)(2,1)}), bf16[2048,512]{1,0:T(8,128)(2,1)}) %all-gather.3.cloned.1.call-update) | async-done | bytes 2097168 | tf_op jit(solution)/shard_map/all_gather | solution.py:116
  152.8 4.0 %copy.116 = bf16[2048,512]{0,1:T(8,128)(2,1)} copy(bf16[2048,512]{1,0:T(8,128)(2,1)} %all-gather.3.cloned.1.call-done) | data formatting | bytes 4194304 | tf_op jit(solution)/shard_map/all_gather | solution.py:116
  156.7 2.7 %slice_bitcast_fusion = (bf16[4,2048,64]{1,2,0:T(8,128)(2,1)}, bf16[4,2048,64]{1,2,0:T(8,128)(2,1)S(1)}) fusion(bf16[2048,4,2,64]{0,3,2,1:T(8,128)(2,1)} %bitcast.207), kind=kLoop, calls=%fused_computation.71 | loop fusion | bytes 4194304 | tf_op jit(solution)/shard_map/transpose | solution.py:42
  159.5 9.9 %while.38 = (s32[]{:T(128)}, f32[4,32,64]{2,1,0:T(8,128)S(1)}, f32[4,32]{1,0:T(4,128)S(1)}, bf16[4,32,64]{2,1,0:T(8,128)(2,1)}, bf16[4,2048,64]{1,2,0:T(8,128)(2...) while((s32[]{:T(128)}, f32[4,32,64]{2,1,0:T(8,128)S(1)}, f32[4,32]{1,0:T(4,128)S(1)}, ...), condition=%wide.region_16.17_spmd, body=%wide.region_13.16_spmd.sunk | while | flops 17172448 | bytes 1339481 | solution.py:37
  171.3 3.9 %fusion.58 = bf16[1024,4,64]{2,0,1:T(8,128)(2,1)S(1)} fusion(f32[1024,4,64]{2,0,1:T(8,128)S(1)} %bitcast.204, f32[4,1024,64]{2,1,0:T(8,128)S(1)} %copy-done.3, f32[1024,4]{0,1:T(4,128)S(1)} %get-tuple-element.236, f32[32,4,64]{2,0,1:T(8,128)S(1)} %bitcast.219, f32[1024,4]{0,1:T(4,128)S(1)} %get-tuple-element.239, f32[1024,4]{0,1:T(4,128)S(1)} %get-tuple-element.237, ...), kind=kLoop, calls=%fused_computation.66 | loop fusion | flops 2359296 | bytes 2727936 | tf_op jit(solution)/shard_map/convert_element_type | solution.py:131
  176.4 31.0 %all-gather.5.cloned.1.call-done = bf16[1024,1024]{0,1:T(8,128)(2,1)} async-done(((bf16[1024,256]{0,1:T(8,128)(2,1)}), bf16[1024,1024]{0,1:T(8,128)(2,1)}) %all-gather.5.cloned.1.call-update) | async-done | bytes 2097168 | tf_op jit(solution)/shard_map/all_gather | solution.py:137
  207.3 3.2 %convolution_convert_fusion = bf16[1024,256]{1,0:T(8,128)(2,1)} fusion(bf16[1024,1024]{0,1:T(8,128)(2,1)} %all-gather.5.cloned.1.call-done, bf16[1024,1024]{1,0:T(8,128)(2,1)S(1)} %copy-done, s32[]{:T(128)S(6)} %select_n.116), kind=kOutput, calls=%fused_computation.67 | convolution fusion | flops 537133056 | bytes 3145732 | tf_op jit(solution)/shard_map/dot_general | solution.py:136
  (162 shorter events, 89.9 us)
Async XLA Ops:
  6.5 200.8 %copy-start = (bf16[1024,1024]{1,0:T(8,128)(2,1)S(1)}, bf16[1024,1024]{1,0:T(8,128)(2,1)}, u32[]{:S(2)}) copy-start(bf16[1024,1024]{1,0:T(8,128)(2,1)} %param.14) | copy-start | bytes 6291460
  6.5 2.2 %copy-start.16 = (bf16[1024]{0:T(1024)(128)(2,1)S(1)}, bf16[1024]{0:T(1024)(128)(2,1)}, u32[]{:S(2)}) copy-start(bf16[1024]{0:T(1024)(128)(2,1)} %param.12) | copy-start | bytes 6148
  6.5 146.2 %all-gather.3.cloned.1.call-start = ((), (), s32[]{:S(2)}) async-start(), calls=%async_computation | async-start | bytes 2129920 | tf_op jit(solution)/shard_map/all_gather | solution.py:116
  6.5 2.4 %copy-start.10 = (bf16[1024,1024]{1,0:T(8,128)(2,1)S(1)}, bf16[1024,1024]{1,0:T(8,128)(2,1)}, u32[]{:S(2)}) copy-start(bf16[1024,1024]{1,0:T(8,128)(2,1)} %param.11) | copy-start | bytes 6291460
  13.1 54.6 %collective-permute-start = (bf16[1024,512]{0,1:T(8,128)(2,1)S(1)}, bf16[1024,512]{0,1:T(8,128)(2,1)}, u32[]{:S(2)}, u32[]{:S(2)}) collective-permute-start(bf16[1024,512]{0,1:T(8,128)(2,1)S(1)} %bitcast.203), channel_id=1, source_target_pairs={{0,4},{4,0},{8,12},{12,8},{16,20},{20,16},{24,28},{28,24},{32,36},... | collective-permute-start | bytes 3145736 | tf_op jit(solution)/shard_map/ppermute | solution.py:15
  20.3 5.1 %copy-start.17 = (s32[4,2]{0,1:T(2,128)S(1)}, s32[4,2]{0,1:T(2,128)}, u32[]{:S(2)}) copy-start(s32[4,2]{0,1:T(2,128)} %param.15) | copy-start | bytes 100
  29.4 8.6 %copy-start.12 = (bf16[256,4,128]{0,2,1:T(8,128)(2,1)}, bf16[256,4,128]{0,2,1:T(8,128)(2,1)S(1)}, u32[]{:S(2)}) copy-start(bf16[256,4,128]{0,2,1:T(8,128)(2,1)S(1)} %copy.123) | copy-start | bytes 786436
  29.4 11.2 %collective-permute-start.1 = (bf16[256,512]{0,1:T(8,128)(2,1)S(1)}, bf16[256,512]{0,1:T(8,128)(2,1)}, u32[]{:S(2)}, u32[]{:S(2)}) collective-permute-start(bf16[256,512]{0,1:T(8,128)(2,1)S(1)} %bitcast.211), channel_id=1, source_target_pairs={{0,4},{4,0},{8,12},{12,8},{16,20},{20,16},{24,28},{28,24},{32,36},... | collective-permute-start | bytes 786440 | tf_op jit(solution)/shard_map/ppermute | solution.py:15
  40.5 166.8 %all-gather.5.cloned.1.call-start = ((), (), s32[]{:S(2)}) async-start(), calls=%async_computation.1 | async-start | bytes 2621440 | tf_op jit(solution)/shard_map/all_gather | solution.py:137
  40.6 2.8 %copy-start.11 = (bf16[1024,1024]{1,0:T(8,128)(2,1)S(1)}, bf16[1024,1024]{1,0:T(8,128)(2,1)}, u32[]{:S(2)}) copy-start(bf16[1024,1024]{1,0:T(8,128)(2,1)} %param.11) | copy-start | bytes 6291460
  43.4 18.0 %collective-permute-start.2 = (bf16[512,512]{0,1:T(8,128)(2,1)}, bf16[512,512]{0,1:T(8,128)(2,1)}, u32[]{:S(2)}, u32[]{:S(2)}) collective-permute-start(bf16[512,512]{0,1:T(8,128)(2,1)} %pad_maximum_fusion.4), channel_id=1, source_target_pairs={{0,8},{4,12},{8,0},{12,4},{16,24},{20,28},{24,16},{28,20},{32,40},... | collective-permute-start | bytes 1572872 | tf_op jit(solution)/shard_map/ppermute | solution.py:15
  56.3 3.1 %copy-start.8 = (bf16[32,32,4,64]{3,2,1,0:T(4,128)(2,1)S(1)}, bf16[32,32,4,64]{3,2,1,0:T(4,128)(2,1)}, u32[]{:S(2)}) copy-start(bf16[32,32,4,64]{3,2,1,0:T(4,128)(2,1)} %reshape_reshape.18) | copy-start | bytes 1572868
  62.8 2.0 copy-start.6
  64.8 53.9 %collective-permute-start.3 = (bf16[1024,512]{0,1:T(8,128)(2,1)}, bf16[1024,512]{0,1:T(8,128)(2,1)}, u32[]{:S(2)}, u32[]{:S(2)}) collective-permute-start(bf16[1024,512]{0,1:T(8,128)(2,1)} %pad_maximum_fusion.3), channel_id=1, source_target_pairs={{0,16},{4,20},{8,24},{12,28},{16,0},{20,4},{24,8},{28,12},{32,48},... | collective-permute-start | bytes 3145736 | tf_op jit(solution)/shard_map/ppermute | solution.py:15
  72.7 3.2 %copy-start.1 = (f32[1024,2048]{1,0:T(8,128)}, f32[1024,2048]{1,0:T(8,128)S(1)}, u32[]{:S(2)}) copy-start(f32[1024,2048]{1,0:T(8,128)S(1)} %get-tuple-element.371) | copy-start | bytes 25165828 | tf_op jit(solution)/shard_map/while
  83.9 3.2 %copy-start.1 = (f32[1024,2048]{1,0:T(8,128)}, f32[1024,2048]{1,0:T(8,128)S(1)}, u32[]{:S(2)}) copy-start(f32[1024,2048]{1,0:T(8,128)S(1)} %get-tuple-element.371) | copy-start | bytes 25165828 | tf_op jit(solution)/shard_map/while
  95.2 3.2 %copy-start.1 = (f32[1024,2048]{1,0:T(8,128)}, f32[1024,2048]{1,0:T(8,128)S(1)}, u32[]{:S(2)}) copy-start(f32[1024,2048]{1,0:T(8,128)S(1)} %get-tuple-element.371) | copy-start | bytes 25165828 | tf_op jit(solution)/shard_map/while
  106.4 3.2 %copy-start.1 = (f32[1024,2048]{1,0:T(8,128)}, f32[1024,2048]{1,0:T(8,128)S(1)}, u32[]{:S(2)}) copy-start(f32[1024,2048]{1,0:T(8,128)S(1)} %get-tuple-element.371) | copy-start | bytes 25165828 | tf_op jit(solution)/shard_map/while
  115.4 3.3 %copy-start.5 = (bf16[512,512]{0,1:T(8,128)(2,1)S(1)}, bf16[512,512]{0,1:T(8,128)(2,1)}, u32[]{:S(2)}) copy-start(bf16[512,512]{0,1:T(8,128)(2,1)} %copy-done.4) | copy-start | bytes 1572868
  115.4 3.3 %copy-start.7 = (bf16[512,512]{0,1:T(8,128)(2,1)S(1)}, bf16[512,512]{0,1:T(8,128)(2,1)}, u32[]{:S(2)}) copy-start(bf16[512,512]{0,1:T(8,128)(2,1)} %copy-done.6) | copy-start | bytes 1572868
  128.7 1.3 copy-start.2
  134.1 1.3 copy-start.2
  156.7 2.7 %copy-start.14 = (f32[4,32,64]{2,1,0:T(8,128)S(1)}, f32[4,32,64]{2,1,0:T(8,128)}, u32[]{:S(2)}) copy-start(f32[4,32,64]{2,1,0:T(8,128)} %custom-call.4) | copy-start | bytes 98308
  169.6 1.8 copy-start.3
  (6 other events, 6.5 us)
Sparse Core Ops, SparseCore 0:
  40.7 112.0 all-gather.2
  176.5 30.8 all-gather.4
where the time goes:
time: 219 us; the launch traced here: 217 us
  matrix products  65 us (30%)
  local copies, waits for them, and re-layouts  60.7 us (28%)
  waiting for transfers between devices  38.8 us (18%)
  other arithmetic  32.6 us (15%)
  between operations  13.7 us (6%)
  starting transfers between devices  6.37 us (3%)
    dot_general x12, matrix products, attend_head(): jnp.dot(weights.astype(jnp.bfloat16), value_rows, preferred_element_type=...  36.1 us
    all_gather x1, waiting for transfers between devices, shards(): lax.all_gather(attention, 'head', axis=1, tiled=True)  31 us
    dot_general x12, matrix products, attend_head(): jnp.dot(queries, key_rows.T, preferred_element_type=jnp.float32)  18.9 us
    another operation x4, local copies, waits for them, and re-layouts, strided(): values_in.reshape(row_count // dilation, dilation, head_count, features)  15.4 us
    reduce_sum x12, other arithmetic, attend_head(): row_total = jnp.sum(weights, axis=1, keepdims=True)  10.4 us
    while x16, local copies, waits for them, and re-layouts  10.3 us
    all_gather x1, waiting for transfers between devices, shards(): far_keys = lax.all_gather(far_local, 'seg', axis=0, tiled=True)  7.83 us
    reduce_sum x4, other arithmetic, strided(): return jnp.sum(grouped * chosen[None, :, :, None], axis=1)  7.79 us
  transfers between devices with their start and end apart: 6, of which 2 were waited for; matrix products, arithmetic and copies ran while one was open for 52% of the time, Pallas kernels for 0%

commit v1 on v0

v1 whole, which is shorter than its diff:
```python
import functools

import jax
import jax.numpy as jnp
from jax import lax
from jax.experimental import pallas as pl
from jax.experimental.pallas import tpu as pltpu
from jax.sharding import PartitionSpec as P

HEAD_DIM = 64
MID_RATE = 4
FAR_RATE = 32
EPS = 1e-06
LANES = 128
BF = jnp.bfloat16
F32 = jnp.float32
SCALE = 1.4426950408889634 * HEAD_DIM ** (-0.5)
VMEM = pl.BlockSpec(memory_space=pltpu.VMEM)
SMEM = pl.BlockSpec(memory_space=pltpu.SMEM)
PARAMS = pltpu.CompilerParams(vmem_limit_bytes=56 * 2**20)


def shape(rows, columns, dtype=BF):
    return jax.ShapeDtypeStruct((rows, columns), dtype)


def left_lanes():
    return lax.broadcasted_iota(jnp.int32, (1, LANES), 1) < HEAD_DIM


def project_kernel(
    offsets, tokens, gain, weight, q_out, kv0_out, kv1_out, qm_out, kvm_out, qf_out, kvf_out, held
):
    rows = tokens.shape[0]
    x = tokens[...].astype(F32)
    mean_square = jnp.mean(x * x, axis=1, keepdims=True)
    normed = (x * lax.rsqrt(mean_square + EPS) * gain[...].astype(F32)).astype(BF)
    near = (kv0_out, kv1_out)
    for part in range(3):
        y = jnp.dot(normed, weight[part], preferred_element_type=F32)
        yb = y.astype(BF)
        for pair in range(2):
            held[2 * part + pair] = y[:, pair * LANES : (pair + 1) * LANES]
        if part == 0:
            q_out[...] = yb
        else:
            for pair in range(2):
                near[pair][:, (part - 1) * LANES : part * LANES] = yb[
                    :, pair * LANES : (pair + 1) * LANES
                ]
    left = left_lanes()
    for rate, which, q_to, kv_to in ((MID_RATE, 0, qm_out, kvm_out), (FAR_RATE, 1, qf_out, kvf_out)):
        count = rows // rate
        for pair in range(2):
            o0 = offsets[2 * pair, which]
            o1 = offsets[2 * pair + 1, which]
            for part in range(3):
                source = held.at[2 * part + pair]
                a = source[pl.ds(o0, count, stride=rate), :]
                b = source[pl.ds(o1, count, stride=rate), :]
                picked = jnp.where(left, a, b).astype(BF)
                if part == 0:
                    q_to[:, pair * LANES : (pair + 1) * LANES] = picked
                else:
                    c = (2 * pair + part - 1) * LANES
                    kv_to[:, c : c + LANES] = picked


def project(offsets, tokens, gain, weight):
    rows, width = tokens.shape
    own = weight.shape[2]
    block = 512

    def rowed(count, columns):
        return pl.BlockSpec((count, columns), lambda i: (i, 0))

    mid, far = block // MID_RATE, block // FAR_RATE
    return pl.pallas_call(
        project_kernel,
        grid=(rows // block,),
        out_shape=[
            shape(rows, own),
            shape(rows, own),
            shape(rows, own),
            shape(rows // MID_RATE, own),
            shape(rows // MID_RATE, 2 * own),
            shape(rows // FAR_RATE, own),
            shape(rows // FAR_RATE, 2 * own),
        ],
        in_specs=[
            SMEM,
            rowed(block, width),
            pl.BlockSpec((1, width), lambda i: (0, 0)),
            pl.BlockSpec((3, width, own), lambda i: (0, 0, 0)),
        ],
        out_specs=[
            rowed(block, own),
            rowed(block, own),
            rowed(block, own),
            rowed(mid, own),
            rowed(mid, 2 * own),
            rowed(far, own),
            rowed(far, 2 * own),
        ],
        scratch_shapes=[pltpu.VMEM((6, block, LANES), F32)],
        compiler_params=PARAMS,
    )(offsets, tokens, gain.reshape(1, width), weight)


def fill(keys, values, at, key_rows, value_rows):
    left = left_lanes()
    count = key_rows.shape[0]
    one = jnp.ones_like(value_rows)
    keys[:, at : at + count] = jnp.concatenate([key_rows, key_rows], axis=1).T
    values[0, at : at + count, :] = jnp.where(left, value_rows, one)
    values[1, at : at + count, :] = jnp.where(left, one, value_rows)


def attend(q, head, keys, values):
    left = left_lanes()
    scaled = q.astype(F32) * SCALE
    scaled = jnp.where(left, scaled, 0.0) if head == 0 else jnp.where(left, 0.0, scaled)
    high = scaled.astype(BF)
    low = (scaled - high.astype(F32)).astype(BF)
    scores = jnp.dot(jnp.concatenate([high, low], axis=1), keys[...], preferred_element_type=F32)
    peak = jnp.max(scores, axis=1, keepdims=True)
    weights = jnp.exp2(scores - peak).astype(BF)
    return jnp.dot(weights, values[head], preferred_element_type=F32), peak


def near_kernel(q, own, theirs, acc_out, peak_out, keys, values):
    rows = q.shape[0]
    block = 256
    for i, kv in enumerate((own, theirs)):
        fill(keys, values, i * rows, kv[:, :LANES], kv[:, LANES:])

    def step(r, _):
        at = pl.ds(pl.multiple_of(r * block, block), block)
        for head in range(2):
            acc, peak = attend(q[at, :], head, keys, values)
            acc_out[head, at, :] = acc
            peak_out[head, at, :] = jnp.broadcast_to(peak, (block, LANES))
        return 0

    lax.fori_loop(0, rows // block, step, 0)


def near_attention(q, pair, own, theirs):
    rows = q.shape[0]
    return pl.pallas_call(
        near_kernel,
        grid=(1,),
        out_shape=[jax.ShapeDtypeStruct((2, rows, LANES), F32)] * 2,
        in_specs=[
            pl.BlockSpec((rows, LANES), lambda i: (0, pair)),
            pl.BlockSpec((rows, 2 * LANES), lambda i: (0, 0)),
            pl.BlockSpec((rows, 2 * LANES), lambda i: (0, 0)),
        ],
        out_specs=[pl.BlockSpec((2, rows, LANES), lambda i: (0, 0, 0))] * 2,
        scratch_shapes=[
            pltpu.VMEM((2 * LANES, 2 * rows), BF),
            pltpu.VMEM((2, 2 * rows, LANES), BF),
        ],
        compiler_params=PARAMS,
        cost_estimate=pl.CostEstimate(flops=8 * 10**9, bytes_accessed=4 * 10**6, transcendentals=0),
    )(q, own, theirs)


def merge_kernel(offsets, qm, qf, *refs):
    mids, fars = refs[0:8], refs[8:16]
    accs_in, peaks_in = refs[16:18], refs[18:20]
    out = refs[20]
    keys, values, acc, peak = refs[21:25]
    left = left_lanes()
    rows = out.shape[0]
    for pair in range(2):
        acc[...] = accs_in[pair][...]
        peak[...] = peaks_in[pair][...]
        lanes = slice(pair * LANES, (pair + 1) * LANES)
        k_at = slice(2 * pair * LANES, (2 * pair + 1) * LANES)
        v_at = slice((2 * pair + 1) * LANES, (2 * pair + 2) * LANES)
        for pieces, q, rate, which in ((mids, qm, MID_RATE, 0), (fars, qf, FAR_RATE, 1)):
            at = 0
            for piece in pieces:
                fill(keys, values, at, piece[:, k_at], piece[:, v_at])
                at += piece.shape[0]
            for head in range(2):
                more, more_peak = attend(q[:, lanes], head, keys, values)
                chosen = pl.ds(offsets[2 * pair + head, which], rows // rate, stride=rate)
                old, old_peak = acc.at[head][chosen, :], peak.at[head][chosen, :]
                top = jnp.maximum(old_peak, more_peak)
                acc.at[head][chosen, :] = old * jnp.exp2(old_peak - top) + more * jnp.exp2(
                    more_peak - top
                )
                peak.at[head][chosen, :] = top
        a, b = acc[0], acc[1]
        total = pltpu.roll(jnp.where(left, b, a), HEAD_DIM, 1)
        out[:, lanes] = (jnp.where(left, a, b) / total).astype(BF)


def merge(offsets, qm, qf, mids, fars, accs, peaks, rows):
    own = qm.shape[1]
    return pl.pallas_call(
        merge_kernel,
        out_shape=shape(rows, own),
        in_specs=[SMEM] + [VMEM] * (2 + 16 + 4),
        out_specs=VMEM,
        scratch_shapes=[
            pltpu.VMEM((2 * LANES, 2048), BF),
            pltpu.VMEM((2, 2048, LANES), BF),
            pltpu.VMEM((2, rows, LANES), F32),
            pltpu.VMEM((2, rows, LANES), F32),
        ],
        compiler_params=PARAMS,
        cost_estimate=pl.CostEstimate(flops=5 * 10**9, bytes_accessed=9 * 10**6, transcendentals=0),
    )(offsets, qm, qf, *mids, *fars, *accs, *peaks)


def out_kernel(me, a0, a1, a2, a3, weight, out):
    total = None
    for d, part in enumerate((a0, a1, a2, a3)):
        depth = part.shape[1]
        at = pl.multiple_of((me[0] ^ d) * depth, depth)
        term = jnp.dot(part[...], weight[pl.ds(at, depth), :], preferred_element_type=F32)
        total = term if total is None else total + term
    out[...] = total.astype(BF)


def project_out(me, parts, weight):
    rows, own = parts[0].shape
    block = 512
    width = weight.shape[0]
    return pl.pallas_call(
        out_kernel,
        out_shape=shape(rows, own),
        grid_spec=pltpu.PrefetchScalarGridSpec(
            num_scalar_prefetch=1,
            grid=(rows // block,),
            in_specs=[pl.BlockSpec((block, own), lambda i, me: (i, 0))] * 4
            + [pl.BlockSpec((width, own), lambda i, me: (0, me[0]))],
            out_specs=pl.BlockSpec((block, own), lambda i, me: (i, 0)),
        ),
        compiler_params=PARAMS,
    )(me, *parts, weight)


def seg_move(array, target):
    pairs = []
    for i in range(64):
        x, z, core = i // 16, i // 2 % 8, i % 2
        x, z, core = target(x, z, core)
        pairs.append((i, (x % 4 * 8 + z % 8) * 2 + core))
    return lax.ppermute(array, "seg", pairs)


def swap_core(array):
    return seg_move(array, lambda x, z, core: (x, z, 1 - core))


def near_z(array, distance):
    return seg_move(array, lambda x, z, core: (x, z ^ distance, core))


def both_ways(array, distance):
    return seg_move(array, lambda x, z, core: (x, z + (distance if core == 0 else -distance), core))


def along_x(array, distance):
    return seg_move(array, lambda x, z, core: (x ^ distance, z, core))


def shards(tokens, norm_gain, qkv_weight, out_weight, offsets):
    rows = tokens.shape[0]
    q, kv0, kv1, qm, kvm, qf, kvf = project(offsets, tokens, norm_gain, qkv_weight)
    other0, other1 = swap_core(kv0), swap_core(kv1)
    chip = jnp.concatenate([kvf, swap_core(kvf)], axis=0)
    line = jnp.concatenate(
        [kvf, both_ways(kvf, 4)] + [both_ways(chip, distance) for distance in (1, 2, 3)], axis=0
    )
    fars = [line] + [along_x(line, distance) for distance in (1, 2, 3)]
    fars = fars + [swap_core(piece) for piece in fars]
    mids = [kvm] + [near_z(kvm, distance) for distance in (1, 2, 3)]
    mids = mids + [swap_core(piece) for piece in mids]
    acc0, peak0 = near_attention(q, 0, kv0, other0)
    acc1, peak1 = near_attention(q, 1, kv1, other1)
    attention = merge(offsets, qm, qf, mids, fars, (acc0, acc1), (peak0, peak1), rows)
    me = lax.axis_index("head").astype(jnp.int32)
    parts = [attention] + [
        lax.ppermute(attention, "head", [(i, i ^ d) for i in range(4)]) for d in (1, 2, 3)
    ]
    return project_out(me.reshape(1), parts, out_weight)


def solution(mesh):
    placed = (P("seg", None), P(), P(None, None, "head"), P(), P("head", None))
    return jax.shard_map(
        shards, mesh=mesh, in_specs=placed, out_specs=P("seg", "head"), check_vma=False
    )
```

time: 219 us -> 130 us (0.59)
  matrix products: 65 us -> 0 us
  local copies, waits for them, and re-layouts: 60.7 us -> 6.01 us
  starting transfers between devices: 6.37 us -> 43.8 us
  Pallas kernels: 0 us -> 36.4 us
  other arithmetic: 32.6 us -> 0 us
  between operations: 13.7 us -> 0.18 us
  waiting for transfers between devices: 38.8 us -> 42.7 us
    dot_general x28 -> x0, matrix products: 65 us -> none  [the longest x12 36.1 us: attend_head(): jnp.dot(weights.astype(jnp.bfloat16), value_rows, preferred_element_type=...]
    ppermute x4 -> x24, waiting for transfers between devices: 0.01 us -> 42.7 us  [the longest x3 25 us: shards(): lax.ppermute(attention, 'head', [(i, i ^ d) for i in range(4)])]
    all_gather x2 -> x0, waiting for transfers between devices: 38.8 us -> none  [the longest x1 31 us: shards(): lax.all_gather(attention, 'head', axis=1, tiled=True)]
    ppermute x4 -> x24, starting transfers between devices: 6.33 us -> 43.8 us  [the longest x21 39.9 us: seg_move(): return lax.ppermute(array, 'seg', pairs)]
    pallas_call x0 -> x5, Pallas kernels: none -> 36.4 us  [the longest x2 18.1 us: near_attention(): pl.pallas_call(near_kernel, grid=(1,), out_shape=[jax.ShapeDtypeStruct((2...]
    reduce_sum x17 -> x0, other arithmetic: 20.4 us -> none  [the longest x12 10.4 us: attend_head(): row_total = jnp.sum(weights, axis=1, keepdims=True)]
    another operation x4 -> x0, local copies, waits for them, and re-layouts: 15.4 us -> none  [strided(): values_in.reshape(row_count // dilation, dilation, head_count, features)]
    while x19 -> x0, local copies, waits for them, and re-layouts: 15 us -> none
  transfers between devices with their start and end apart: 6 -> 24, of which waited for: 2 -> 7; matrix products, arithmetic and copies ran while one was open for 52% -> 1% of each run, Pallas kernels for 0% -> 14%
where the time goes in v1:
time: 130 us; the launch traced here: 129 us
  starting transfers between devices  43.8 us (34%)
  waiting for transfers between devices  42.7 us (33%)
  Pallas kernels  36.4 us (28%)
  local copies, waits for them, and re-layouts  6.01 us (5%)
    ppermute x21, starting transfers between devices, seg_move(): return lax.ppermute(array, 'seg', pairs)  39.9 us
    ppermute x3, waiting for transfers between devices, shards(): lax.ppermute(attention, 'head', [(i, i ^ d) for i in range(4)])  25 us
    pallas_call x2, Pallas kernels, near_attention(): pl.pallas_call(near_kernel, grid=(1,), out_shape=[jax.ShapeDtypeStruct((2...  18.1 us
    ppermute x21, waiting for transfers between devices, seg_move(): return lax.ppermute(array, 'seg', pairs)  17.7 us
    pallas_call x1, Pallas kernels, merge(): pl.pallas_call(merge_kernel, out_shape=shape(rows, own), in_specs=[SMEM]...  10.1 us
    pallas_call x1, Pallas kernels, project(): pl.pallas_call(project_kernel, grid=(rows // block,), out_shape=[shape(ro...  5.15 us
    unnamed x45, local copies, waits for them, and re-layouts  4.72 us
    ppermute x3, starting transfers between devices, shards(): lax.ppermute(attention, 'head', [(i, i ^ d) for i in range(4)])  3.92 us
  transfers between devices with their start and end apart: 24, of which 7 were waited for; matrix products, arithmetic and copies ran while one was open for 1% of the time, Pallas kernels for 14%

profile of v1, /device:TPU:1, one launch (start us, length us, event | category | flops | bytes accessed | tf_op | source)
XLA Modules:
  0.0 129.1 jit_solution(5967001151177763232)
XLA Ops:
  0.0 1.4 %copy.7.offsets = s32[4,2]{1,0:T(4,128)} copy(s32[4,2]{0,1:T(2,128)} %param.9) | data formatting | bytes 64 | tf_op args[4]
  1.4 1.3 reshape.7.gain
  2.6 5.2 %shard_map.55 = (bf16[1024,256]{1,0:T(8,128)(2,1)}, bf16[1024,256]{1,0:T(8,128)(2,1)}, bf16[1024,256]{1,0:T(8,128)(2,1)}, bf16[256,256]{1,0:T(8,128)(2,1)}, bf16...) custom-call(s32[4,2]{1,0:T(4,128)} %copy.7.offsets, bf16[1024,1024]{1,0:T(8,128)(2,1)} %tokens.1, ...), custom_call_target="tpu_custom_call" | custom-call | tf_op jit(solution)/shard_map/pallas_call | solution.py:78
  7.8 3.3 %collective-permute-start.8 = (bf16[32,512]{1,0:T(8,128)(2,1)}, bf16[32,512]{1,0:T(8,128)(2,1)S(1)}, u32[]{:S(2)}, u32[]{:S(2)}) collective-permute-start(bf16[32,512]{1,0:T(8,128)(2,1)} %get-tuple-element.19), channel_id=1, source_target_pairs={{0,4},{4,0},{8,12},{12,8},{16,20},{20,16},{24,28},{28,24},{32,36},... | collective-permute-start | bytes 98312 | tf_op jit(solution)/shard_map/ppermute | solution.py:253
  11.1 5.2 %collective-permute-start.7 = (bf16[32,512]{1,0:T(8,128)(2,1)}, bf16[32,512]{1,0:T(8,128)(2,1)S(1)}, u32[]{:S(2)}, u32[]{:S(2)}) collective-permute-start(bf16[32,512]{1,0:T(8,128)(2,1)} %get-tuple-element.19), channel_id=1, source_target_pairs={{0,32},{4,36},{8,40},{12,44},{16,48},{20,52},{24,56},{28,60},{32,0... | collective-permute-start | bytes 98312 | tf_op jit(solution)/shard_map/ppermute | solution.py:253
  18.2 1.6 %collective-permute-start.2 = (bf16[256,512]{1,0:T(8,128)(2,1)}, bf16[256,512]{1,0:T(8,128)(2,1)S(1)}, u32[]{:S(2)}, u32[]{:S(2)}) collective-permute-start(bf16[256,512]{1,0:T(8,128)(2,1)} %get-tuple-element.18.refs_0_), channel_id=1, source_target_pairs={{0,24},{4,28},{8,16},{12,20},{16,8},{20,12},{24,0},{28,4},{32,56},... | collective-permute-start | bytes 786440 | tf_op jit(solution)/shard_map/ppermute | solution.py:253
  22.0 9.5 %collective-permute-done.9 = bf16[64,512]{1,0:T(8,128)(2,1)S(1)} collective-permute-done((bf16[64,512]{1,0:T(8,128)(2,1)S(1)}, bf16[64,512]{1,0:T(8,128)(2,1)S(1)}, u32[]{:S(2)}, u32[]{:S(2)}) %collective-permute-start.9) | collective-permute-done | bytes 65568 | tf_op jit(solution)/shard_map/ppermute | solution.py:253
  31.5 10.9 %collective-permute-start.10 = (bf16[64,512]{1,0:T(8,128)(2,1)S(1)}, bf16[64,512]{1,0:T(8,128)(2,1)S(1)}, u32[]{:S(2)}, u32[]{:S(2)}) collective-permute-start(bf16[64,512]{1,0:T(8,128)(2,1)S(1)} %constant_dynamic-update-slice_fusion), channel_id=1, source_target_pairs={{0,16},{4,52},{8,24},{12,60},{16,32},{20,4},{24,40},{28,12},{32,48... | collective-permute-start | bytes 196616 | tf_op jit(solution)/shard_map/ppermute | solution.py:253
  42.4 2.2 %collective-permute-done.10 = bf16[64,512]{1,0:T(8,128)(2,1)S(1)} collective-permute-done((bf16[64,512]{1,0:T(8,128)(2,1)S(1)}, bf16[64,512]{1,0:T(8,128)(2,1)S(1)}, u32[]{:S(2)}, u32[]{:S(2)}) %collective-permute-start.10) | collective-permute-done | bytes 65568 | tf_op jit(solution)/shard_map/ppermute | solution.py:253
  44.5 4.5 %collective-permute-start.11 = (bf16[64,512]{1,0:T(8,128)(2,1)S(1)}, bf16[64,512]{1,0:T(8,128)(2,1)S(1)}, u32[]{:S(2)}, u32[]{:S(2)}) collective-permute-start(bf16[64,512]{1,0:T(8,128)(2,1)S(1)} %constant_dynamic-update-slice_fusion), channel_id=1, source_target_pairs={{0,24},{4,44},{8,32},{12,52},{16,40},{20,60},{24,48},{28,4},{32,56... | collective-permute-start | bytes 196616 | tf_op jit(solution)/shard_map/ppermute | solution.py:253
  49.1 2.2 %collective-permute-done.11 = bf16[64,512]{1,0:T(8,128)(2,1)S(1)} collective-permute-done((bf16[64,512]{1,0:T(8,128)(2,1)S(1)}, bf16[64,512]{1,0:T(8,128)(2,1)S(1)}, u32[]{:S(2)}, u32[]{:S(2)}) %collective-permute-start.11) | collective-permute-done | bytes 65568 | tf_op jit(solution)/shard_map/ppermute | solution.py:253
  51.3 4.0 %collective-permute-start.3 = (bf16[256,512]{1,0:T(8,128)(2,1)}, bf16[256,512]{1,0:T(8,128)(2,1)S(1)}, u32[]{:S(2)}, u32[]{:S(2)}) collective-permute-start(bf16[256,512]{1,0:T(8,128)(2,1)} %get-tuple-element.18.refs_0_), channel_id=1, source_target_pairs={{0,4},{4,0},{8,12},{12,8},{16,20},{20,16},{24,28},{28,24},{32,36},... | collective-permute-start | bytes 786440 | tf_op jit(solution)/shard_map/ppermute | solution.py:253
  55.3 1.3 %collective-permute-start.12 = (bf16[256,512]{1,0:T(8,128)(2,1)S(1)}, bf16[256,512]{1,0:T(8,128)(2,1)S(1)}, u32[]{:S(2)}, u32[]{:S(2)}) collective-permute-start(bf16[256,512]{1,0:T(8,128)(2,1)S(1)} %constant_dynamic-update-slice_fusion.2.refs_8_), channel_id=1, source_target_pairs={{0,64},{4,68},{8,72},{12,76},{16,80},{20,84},{24,88},{28,92},{32,9... | collective-permute-start | bytes 786440 | tf_op jit(solution)/shard_map/ppermute | solution.py:253
  56.9 2.5 %collective-permute-start.13 = (bf16[256,512]{1,0:T(8,128)(2,1)S(1)}, bf16[256,512]{1,0:T(8,128)(2,1)S(1)}, u32[]{:S(2)}, u32[]{:S(2)}) collective-permute-start(bf16[256,512]{1,0:T(8,128)(2,1)S(1)} %constant_dynamic-update-slice_fusion.2.refs_8_), channel_id=1, source_target_pairs={{0,128},{4,132},{8,136},{12,140},{16,144},{20,148},{24,152},{28,15... | collective-permute-start | bytes 786440 | tf_op jit(solution)/shard_map/ppermute | solution.py:253
  59.5 3.7 %collective-permute-done.12.refs_9_ = bf16[256,512]{1,0:T(8,128)(2,1)S(1)} collective-permute-done((bf16[256,512]{1,0:T(8,128)(2,1)S(1)}, bf16[256,512]{1,0:T(8,128)(2,1)S(1)}, u32[]{:S(2)}, u32[]{:S(2)}) %collective-permute-start.12) | collective-permute-done | bytes 262176 | tf_op jit(solution)/shard_map/ppermute | solution.py:253
  65.3 9.1 %shard_map.56 = (f32[2,1024,128]{2,1,0:T(8,128)}, f32[2,1024,128]{2,1,0:T(8,128)}) custom-call(bf16[1024,256]{1,0:T(8,128)(2,1)} %get-tuple-element.20.q, bf16[1024,256]{1,0:T(8,128)(2,1)} %get-tuple-element.21.own, bf16[1024,256]{1,0:T(8,128)(2,1)} %copy-done.4), custom_call_target="tpu_custom_call" | custom-call | flops 8000000000 | bytes 4000000 | tf_op jit(solution)/shard_map/pallas_call | solution.py:150
  76.1 9.0 %shard_map.57 = (f32[2,1024,128]{2,1,0:T(8,128)}, f32[2,1024,128]{2,1,0:T(8,128)}) custom-call(bf16[1024,256]{1,0:T(8,128)(2,1)} %get-tuple-element.20.q, bf16[1024,256]{1,0:T(8,128)(2,1)} %get-tuple-element.23.own, bf16[1024,256]{1,0:T(8,128)(2,1)} %copy-done.5), custom_call_target="tpu_custom_call" | custom-call | flops 8000000000 | bytes 4000000 | tf_op jit(solution)/shard_map/pallas_call | solution.py:150
  86.2 10.1 %shard_map.58.a0 = bf16[1024,256]{1,0:T(8,128)(2,1)} custom-call(s32[4,2]{1,0:T(4,128)} %copy.7.offsets, bf16[256,256]{1,0:T(8,128)(2,1)} %get-tuple-element.16.qm, bf16[32,256]{1,0:T(8,128)(2,1)} %get-tuple-element.17.qf, bf16[256,512]{1,0:T(8,128)(2,1)} %get-tuple-element.18.refs_0_, bf16[256,512]{1,0:T(8,128)(2,1)} %copy-done.6, ...), custom_call_target="tpu_custom_call" | custom-call | flops 5000000000 | bytes 9000000 | tf_op jit(solution)/shard_map/pallas_call | solution.py:203
  96.3 1.3 collective-permute-start.21
  97.6 2.6 %collective-permute-start.22 = (bf16[1024,256]{1,0:T(8,128)(2,1)}, bf16[1024,256]{1,0:T(8,128)(2,1)S(1)}, u32[]{:S(2)}, u32[]{:S(2)}) collective-permute-start(bf16[1024,256]{1,0:T(8,128)(2,1)} %shard_map.58.a0), channel_id=1, source_target_pairs={{0,2},{1,3},{2,0},{3,1},{4,6},{5,7},{6,4},{7,5},{8,10},{9,11},{10,... | collective-permute-start | bytes 1572872 | tf_op jit(solution)/shard_map/ppermute | solution.py:289
  100.2 9.3 %collective-permute-done.21.a1 = bf16[1024,256]{1,0:T(8,128)(2,1)S(1)} collective-permute-done((bf16[1024,256]{1,0:T(8,128)(2,1)}, bf16[1024,256]{1,0:T(8,128)(2,1)S(1)}, u32[]{:S(2)}, u32[]{:S(2)}) %collective-permute-start.21) | collective-permute-done | bytes 524320 | tf_op jit(solution)/shard_map/ppermute | solution.py:289
  109.5 13.7 %collective-permute-done.22.a2 = bf16[1024,256]{1,0:T(8,128)(2,1)S(1)} collective-permute-done((bf16[1024,256]{1,0:T(8,128)(2,1)}, bf16[1024,256]{1,0:T(8,128)(2,1)S(1)}, u32[]{:S(2)}, u32[]{:S(2)}) %collective-permute-start.22) | collective-permute-done | bytes 524320 | tf_op jit(solution)/shard_map/ppermute | solution.py:289
  123.3 2.0 %collective-permute-done.23.a3 = bf16[1024,256]{1,0:T(8,128)(2,1)S(1)} collective-permute-done((bf16[1024,256]{1,0:T(8,128)(2,1)}, bf16[1024,256]{1,0:T(8,128)(2,1)S(1)}, u32[]{:S(2)}, u32[]{:S(2)}) %collective-permute-start.23) | collective-permute-done | bytes 524320 | tf_op jit(solution)/shard_map/ppermute | solution.py:289
  126.1 3.1 %shard_map.59 = bf16[1024,256]{1,0:T(8,128)(2,1)} custom-call(s32[1]{0:T(128)} %bitcast.me, bf16[1024,256]{1,0:T(8,128)(2,1)} %shard_map.58.a0, bf16[1024,256]{1,0:T(8,128)(2,1)} %copy-done, bf16[1024,256]{1,0:T(8,128)(2,1)} %copy-done.1, bf16[1024,256]{1,0:T(8,128)(2,1)} %copy-done.2, bf16[1024,1024]{1,0:T(8,128)(2,1)} %weight.3), custom_call_target="tpu_custom_call" | custom-call | tf_op jit(solution)/shard_map/pallas_call | solution.py:233
  (77 shorter events, 10.0 us)
Async XLA Ops:
  7.8 12.8 %collective-permute-start.8 = (bf16[32,512]{1,0:T(8,128)(2,1)}, bf16[32,512]{1,0:T(8,128)(2,1)S(1)}, u32[]{:S(2)}, u32[]{:S(2)}) collective-permute-start(bf16[32,512]{1,0:T(8,128)(2,1)} %get-tuple-element.19), channel_id=1, source_target_pairs={{0,4},{4,0},{8,12},{12,8},{16,20},{20,16},{24,28},{28,24},{32,36},... | collective-permute-start | bytes 98312 | tf_op jit(solution)/shard_map/ppermute | solution.py:253
  11.1 10.7 %collective-permute-start.7 = (bf16[32,512]{1,0:T(8,128)(2,1)}, bf16[32,512]{1,0:T(8,128)(2,1)S(1)}, u32[]{:S(2)}, u32[]{:S(2)}) collective-permute-start(bf16[32,512]{1,0:T(8,128)(2,1)} %get-tuple-element.19), channel_id=1, source_target_pairs={{0,32},{4,36},{8,40},{12,44},{16,48},{20,52},{24,56},{28,60},{32,0... | collective-permute-start | bytes 98312 | tf_op jit(solution)/shard_map/ppermute | solution.py:253
  16.3 39.0 %collective-permute-start = (bf16[256,512]{1,0:T(8,128)(2,1)}, bf16[256,512]{1,0:T(8,128)(2,1)S(1)}, u32[]{:S(2)}, u32[]{:S(2)}) collective-permute-start(bf16[256,512]{1,0:T(8,128)(2,1)} %get-tuple-element.18.refs_0_), channel_id=1, source_target_pairs={{0,8},{4,12},{8,0},{12,4},{16,24},{20,28},{24,16},{28,20},{32,40},... | collective-permute-start | bytes 786440 | tf_op jit(solution)/shard_map/ppermute | solution.py:253
  17.0 39.5 %collective-permute-start.1 = (bf16[256,512]{1,0:T(8,128)(2,1)}, bf16[256,512]{1,0:T(8,128)(2,1)S(1)}, u32[]{:S(2)}, u32[]{:S(2)}) collective-permute-start(bf16[256,512]{1,0:T(8,128)(2,1)} %get-tuple-element.18.refs_0_), channel_id=1, source_target_pairs={{0,16},{4,20},{8,24},{12,28},{16,0},{20,4},{24,8},{28,12},{32,48},... | collective-permute-start | bytes 786440 | tf_op jit(solution)/shard_map/ppermute | solution.py:253
  18.2 38.6 %collective-permute-start.2 = (bf16[256,512]{1,0:T(8,128)(2,1)}, bf16[256,512]{1,0:T(8,128)(2,1)S(1)}, u32[]{:S(2)}, u32[]{:S(2)}) collective-permute-start(bf16[256,512]{1,0:T(8,128)(2,1)} %get-tuple-element.18.refs_0_), channel_id=1, source_target_pairs={{0,24},{4,28},{8,16},{12,20},{16,8},{20,12},{24,0},{28,4},{32,56},... | collective-permute-start | bytes 786440 | tf_op jit(solution)/shard_map/ppermute | solution.py:253
  20.6 43.9 %collective-permute-start.19 = (bf16[1024,256]{1,0:T(8,128)(2,1)}, bf16[1024,256]{1,0:T(8,128)(2,1)S(1)}, u32[]{:S(2)}, u32[]{:S(2)}) collective-permute-start(bf16[1024,256]{1,0:T(8,128)(2,1)} %get-tuple-element.21.own), channel_id=1, source_target_pairs={{0,4},{4,0},{8,12},{12,8},{16,20},{20,16},{24,28},{28,24},{32,36},... | collective-permute-start | bytes 1572872 | tf_op jit(solution)/shard_map/ppermute | solution.py:253
  21.8 9.7 %collective-permute-start.9 = (bf16[64,512]{1,0:T(8,128)(2,1)S(1)}, bf16[64,512]{1,0:T(8,128)(2,1)S(1)}, u32[]{:S(2)}, u32[]{:S(2)}) collective-permute-start(bf16[64,512]{1,0:T(8,128)(2,1)S(1)} %constant_dynamic-update-slice_fusion), channel_id=1, source_target_pairs={{0,8},{4,60},{8,16},{12,4},{16,24},{20,12},{24,32},{28,20},{32,40}... | collective-permute-start | bytes 196616 | tf_op jit(solution)/shard_map/ppermute | solution.py:253
  31.5 13.1 %collective-permute-start.10 = (bf16[64,512]{1,0:T(8,128)(2,1)S(1)}, bf16[64,512]{1,0:T(8,128)(2,1)S(1)}, u32[]{:S(2)}, u32[]{:S(2)}) collective-permute-start(bf16[64,512]{1,0:T(8,128)(2,1)S(1)} %constant_dynamic-update-slice_fusion), channel_id=1, source_target_pairs={{0,16},{4,52},{8,24},{12,60},{16,32},{20,4},{24,40},{28,12},{32,48... | collective-permute-start | bytes 196616 | tf_op jit(solution)/shard_map/ppermute | solution.py:253
  44.5 6.7 %collective-permute-start.11 = (bf16[64,512]{1,0:T(8,128)(2,1)S(1)}, bf16[64,512]{1,0:T(8,128)(2,1)S(1)}, u32[]{:S(2)}, u32[]{:S(2)}) collective-permute-start(bf16[64,512]{1,0:T(8,128)(2,1)S(1)} %constant_dynamic-update-slice_fusion), channel_id=1, source_target_pairs={{0,24},{4,44},{8,32},{12,52},{16,40},{20,60},{24,48},{28,4},{32,56... | collective-permute-start | bytes 196616 | tf_op jit(solution)/shard_map/ppermute | solution.py:253
  51.3 8.1 %collective-permute-start.3 = (bf16[256,512]{1,0:T(8,128)(2,1)}, bf16[256,512]{1,0:T(8,128)(2,1)S(1)}, u32[]{:S(2)}, u32[]{:S(2)}) collective-permute-start(bf16[256,512]{1,0:T(8,128)(2,1)} %get-tuple-element.18.refs_0_), channel_id=1, source_target_pairs={{0,4},{4,0},{8,12},{12,8},{16,20},{20,16},{24,28},{28,24},{32,36},... | collective-permute-start | bytes 786440 | tf_op jit(solution)/shard_map/ppermute | solution.py:253
  55.3 8.0 %collective-permute-start.12 = (bf16[256,512]{1,0:T(8,128)(2,1)S(1)}, bf16[256,512]{1,0:T(8,128)(2,1)S(1)}, u32[]{:S(2)}, u32[]{:S(2)}) collective-permute-start(bf16[256,512]{1,0:T(8,128)(2,1)S(1)} %constant_dynamic-update-slice_fusion.2.refs_8_), channel_id=1, source_target_pairs={{0,64},{4,68},{8,72},{12,76},{16,80},{20,84},{24,88},{28,92},{32,9... | collective-permute-start | bytes 786440 | tf_op jit(solution)/shard_map/ppermute | solution.py:253
  56.6 18.7 %collective-permute-start.20 = (bf16[1024,256]{1,0:T(8,128)(2,1)}, bf16[1024,256]{1,0:T(8,128)(2,1)S(1)}, u32[]{:S(2)}, u32[]{:S(2)}) collective-permute-start(bf16[1024,256]{1,0:T(8,128)(2,1)} %get-tuple-element.23.own), channel_id=1, source_target_pairs={{0,4},{4,0},{8,12},{12,8},{16,20},{20,16},{24,28},{28,24},{32,36},... | collective-permute-start | bytes 1572872 | tf_op jit(solution)/shard_map/ppermute | solution.py:253
  56.9 17.5 %collective-permute-start.13 = (bf16[256,512]{1,0:T(8,128)(2,1)S(1)}, bf16[256,512]{1,0:T(8,128)(2,1)S(1)}, u32[]{:S(2)}, u32[]{:S(2)}) collective-permute-start(bf16[256,512]{1,0:T(8,128)(2,1)S(1)} %constant_dynamic-update-slice_fusion.2.refs_8_), channel_id=1, source_target_pairs={{0,128},{4,132},{8,136},{12,140},{16,144},{20,148},{24,152},{28,15... | collective-permute-start | bytes 786440 | tf_op jit(solution)/shard_map/ppermute | solution.py:253
  59.3 15.2 %collective-permute-start.14 = (bf16[256,512]{1,0:T(8,128)(2,1)S(1)}, bf16[256,512]{1,0:T(8,128)(2,1)S(1)}, u32[]{:S(2)}, u32[]{:S(2)}) collective-permute-start(bf16[256,512]{1,0:T(8,128)(2,1)S(1)} %constant_dynamic-update-slice_fusion.2.refs_8_), channel_id=1, source_target_pairs={{0,192},{4,196},{8,200},{12,204},{16,208},{20,212},{24,216},{28,22... | collective-permute-start | bytes 786440 | tf_op jit(solution)/shard_map/ppermute | solution.py:253
  63.3 11.8 %collective-permute-start.15 = (bf16[256,512]{1,0:T(8,128)(2,1)S(1)}, bf16[256,512]{1,0:T(8,128)(2,1)S(1)}, u32[]{:S(2)}, u32[]{:S(2)}) collective-permute-start(bf16[256,512]{1,0:T(8,128)(2,1)S(1)} %constant_dynamic-update-slice_fusion.2.refs_8_), channel_id=1, source_target_pairs={{0,4},{4,0},{8,12},{12,8},{16,20},{20,16},{24,28},{28,24},{32,36},... | collective-permute-start | bytes 786440 | tf_op jit(solution)/shard_map/ppermute | solution.py:253
  64.5 11.2 %collective-permute-start.4 = (bf16[256,512]{1,0:T(8,128)(2,1)S(1)}, bf16[256,512]{1,0:T(8,128)(2,1)S(1)}, u32[]{:S(2)}, u32[]{:S(2)}) collective-permute-start(bf16[256,512]{1,0:T(8,128)(2,1)S(1)} %collective-permute-done.refs_1_), channel_id=1, source_target_pairs={{0,4},{4,0},{8,12},{12,8},{16,20},{20,16},{24,28},{28,24},{32,36},... | collective-permute-start | bytes 786440 | tf_op jit(solution)/shard_map/ppermute | solution.py:253
  74.4 10.7 %collective-permute-start.5 = (bf16[256,512]{1,0:T(8,128)(2,1)S(1)}, bf16[256,512]{1,0:T(8,128)(2,1)S(1)}, u32[]{:S(2)}, u32[]{:S(2)}) collective-permute-start(bf16[256,512]{1,0:T(8,128)(2,1)S(1)} %collective-permute-done.1.refs_2_), channel_id=1, source_target_pairs={{0,4},{4,0},{8,12},{12,8},{16,20},{20,16},{24,28},{28,24},{32,36},... | collective-permute-start | bytes 786440 | tf_op jit(solution)/shard_map/ppermute | solution.py:253
  74.6 10.6 %collective-permute-start.6 = (bf16[256,512]{1,0:T(8,128)(2,1)S(1)}, bf16[256,512]{1,0:T(8,128)(2,1)S(1)}, u32[]{:S(2)}, u32[]{:S(2)}) collective-permute-start(bf16[256,512]{1,0:T(8,128)(2,1)S(1)} %collective-permute-done.2.refs_3_), channel_id=1, source_target_pairs={{0,4},{4,0},{8,12},{12,8},{16,20},{20,16},{24,28},{28,24},{32,36},... | collective-permute-start | bytes 786440 | tf_op jit(solution)/shard_map/ppermute | solution.py:253
  75.1 10.1 %collective-permute-start.16 = (bf16[256,512]{1,0:T(8,128)(2,1)S(1)}, bf16[256,512]{1,0:T(8,128)(2,1)S(1)}, u32[]{:S(2)}, u32[]{:S(2)}) collective-permute-start(bf16[256,512]{1,0:T(8,128)(2,1)S(1)} %collective-permute-done.12.refs_9_), channel_id=1, source_target_pairs={{0,4},{4,0},{8,12},{12,8},{16,20},{20,16},{24,28},{28,24},{32,36},... | collective-permute-start | bytes 786440 | tf_op jit(solution)/shard_map/ppermute | solution.py:253
  75.2 10.0 %collective-permute-start.17 = (bf16[256,512]{1,0:T(8,128)(2,1)S(1)}, bf16[256,512]{1,0:T(8,128)(2,1)S(1)}, u32[]{:S(2)}, u32[]{:S(2)}) collective-permute-start(bf16[256,512]{1,0:T(8,128)(2,1)S(1)} %collective-permute-done.13.refs_10_), channel_id=1, source_target_pairs={{0,4},{4,0},{8,12},{12,8},{16,20},{20,16},{24,28},{28,24},{32,36},... | collective-permute-start | bytes 786440 | tf_op jit(solution)/shard_map/ppermute | solution.py:253
  75.7 9.5 %collective-permute-start.18 = (bf16[256,512]{1,0:T(8,128)(2,1)S(1)}, bf16[256,512]{1,0:T(8,128)(2,1)S(1)}, u32[]{:S(2)}, u32[]{:S(2)}) collective-permute-start(bf16[256,512]{1,0:T(8,128)(2,1)S(1)} %collective-permute-done.14.refs_11_), channel_id=1, source_target_pairs={{0,4},{4,0},{8,12},{12,8},{16,20},{20,16},{24,28},{28,24},{32,36},... | collective-permute-start | bytes 786440 | tf_op jit(solution)/shard_map/ppermute | solution.py:253
  96.3 13.2 %collective-permute-start.21 = (bf16[1024,256]{1,0:T(8,128)(2,1)}, bf16[1024,256]{1,0:T(8,128)(2,1)S(1)}, u32[]{:S(2)}, u32[]{:S(2)}) collective-permute-start(bf16[1024,256]{1,0:T(8,128)(2,1)} %shard_map.58.a0), channel_id=1, source_target_pairs={{0,1},{1,0},{2,3},{3,2},{4,5},{5,4},{6,7},{7,6},{8,9},{9,8},{10,11... | collective-permute-start | bytes 1572872 | tf_op jit(solution)/shard_map/ppermute | solution.py:289
  97.6 25.7 %collective-permute-start.22 = (bf16[1024,256]{1,0:T(8,128)(2,1)}, bf16[1024,256]{1,0:T(8,128)(2,1)S(1)}, u32[]{:S(2)}, u32[]{:S(2)}) collective-permute-start(bf16[1024,256]{1,0:T(8,128)(2,1)} %shard_map.58.a0), channel_id=1, source_target_pairs={{0,2},{1,3},{2,0},{3,1},{4,6},{5,7},{6,4},{7,5},{8,10},{9,11},{10,... | collective-permute-start | bytes 1572872 | tf_op jit(solution)/shard_map/ppermute | solution.py:289
  100.2 25.0 %collective-permute-start.23 = (bf16[1024,256]{1,0:T(8,128)(2,1)}, bf16[1024,256]{1,0:T(8,128)(2,1)S(1)}, u32[]{:S(2)}, u32[]{:S(2)}) collective-permute-start(bf16[1024,256]{1,0:T(8,128)(2,1)} %shard_map.58.a0), channel_id=1, source_target_pairs={{0,3},{1,2},{2,1},{3,0},{4,7},{5,6},{6,5},{7,4},{8,11},{9,10},{10,... | collective-permute-start | bytes 1572872 | tf_op jit(solution)/shard_map/ppermute | solution.py:289
  (20 other events, 165.7 us)

commit v2 on v1

v2 whole, which is shorter than its diff:
```python
import functools

import jax
import jax.numpy as jnp
from jax import lax
from jax.experimental import pallas as pl
from jax.experimental.pallas import tpu as pltpu
from jax.sharding import PartitionSpec as P

HEAD_DIM = 64
MID_RATE = 4
FAR_RATE = 32
GROUP = 2048
EPS = 1e-06
LANES = 128
BF = jnp.bfloat16
F32 = jnp.float32
SCALE = 1.4426950408889634 * HEAD_DIM ** (-0.5)
VMEM = pl.BlockSpec(memory_space=pltpu.VMEM)
SMEM = pl.BlockSpec(memory_space=pltpu.SMEM)
ANY = pl.BlockSpec(memory_space=pl.ANY)
PARAMS = pltpu.CompilerParams(vmem_limit_bytes=56 * 2**20)


def shape(*dims, dtype=BF):
    return jax.ShapeDtypeStruct(dims, dtype)


def left_lanes():
    return lax.broadcasted_iota(jnp.int32, (1, LANES), 1) < HEAD_DIM


def cost(flops, bytes_accessed):
    return pl.CostEstimate(flops=flops, bytes_accessed=bytes_accessed, transcendentals=0)


def project_kernel(
    offsets, tokens, gain, weight, q_out, kv0_out, kv1_out, qm_out, kvm_out, qf_out, kvf_out, held
):
    rows = tokens.shape[0]
    x = tokens[...].astype(F32)
    mean_square = jnp.mean(x * x, axis=1, keepdims=True)
    normed = (x * lax.rsqrt(mean_square + EPS) * gain[...].astype(F32)[None, :]).astype(BF)
    near = (kv0_out, kv1_out)
    for part in range(3):
        y = jnp.dot(normed, weight[part], preferred_element_type=F32)
        yb = y.astype(BF)
        for pair in range(2):
            held[2 * part + pair] = y[:, pair * LANES : (pair + 1) * LANES]
        if part == 0:
            q_out[...] = yb
        else:
            for pair in range(2):
                near[pair][:, (part - 1) * LANES : part * LANES] = yb[
                    :, pair * LANES : (pair + 1) * LANES
                ]
    left = left_lanes()
    for rate, which, q_to, kv_to in ((MID_RATE, 0, qm_out, kvm_out), (FAR_RATE, 1, qf_out, kvf_out)):
        count = rows // rate
        for pair in range(2):
            o0 = offsets[2 * pair, which]
            o1 = offsets[2 * pair + 1, which]
            for part in range(3):
                source = held.at[2 * part + pair]
                a = source[pl.ds(o0, count, stride=rate), :]
                b = source[pl.ds(o1, count, stride=rate), :]
                picked = jnp.where(left, a, b).astype(BF)
                if part == 0:
                    q_to[:, pair * LANES : (pair + 1) * LANES] = picked
                else:
                    c = (2 * pair + part - 1) * LANES
                    kv_to[:, c : c + LANES] = picked


def project(offsets, tokens, gain, weight):
    rows, width = tokens.shape
    own = weight.shape[2]
    block = 512

    def rowed(count, columns):
        return pl.BlockSpec((count, columns), lambda i: (i, 0))

    mid, far = block // MID_RATE, block // FAR_RATE
    return pl.pallas_call(
        project_kernel,
        grid=(rows // block,),
        out_shape=[
            shape(rows, own),
            shape(rows, own),
            shape(rows, own),
            shape(rows // MID_RATE, own),
            shape(rows // MID_RATE, 2 * own),
            shape(rows // FAR_RATE, own),
            shape(rows // FAR_RATE, 2 * own),
        ],
        in_specs=[
            SMEM,
            rowed(block, width),
            pl.BlockSpec((width,), lambda i: (0,)),
            pl.BlockSpec((3, width, own), lambda i: (0, 0, 0)),
        ],
        out_specs=[
            rowed(block, own),
            rowed(block, own),
            rowed(block, own),
            rowed(mid, own),
            rowed(mid, 2 * own),
            rowed(far, own),
            rowed(far, 2 * own),
        ],
        scratch_shapes=[pltpu.VMEM((6, block, LANES), F32)],
        compiler_params=PARAMS,
        cost_estimate=cost(2 * 10**9, 6 * 10**6),
    )(offsets, tokens, gain, weight)


def fill(keys, values, at, key_rows, value_rows):
    left = left_lanes()
    count = key_rows.shape[0]
    one = jnp.ones_like(value_rows)
    turned = key_rows.T
    for head in range(2):
        half = turned[head * HEAD_DIM : (head + 1) * HEAD_DIM]
        keys[head, :HEAD_DIM, at : at + count] = half
        keys[head, HEAD_DIM:, at : at + count] = half
    values[0, at : at + count, :] = jnp.where(left, value_rows, one)
    values[1, at : at + count, :] = jnp.where(left, one, value_rows)


def split_queries(q, head):
    left = left_lanes()
    scaled = q.astype(F32) * SCALE
    high = scaled.astype(BF).astype(F32)
    low = scaled - high
    if head == 0:
        both = jnp.where(left, high, pltpu.roll(low, HEAD_DIM, 1))
    else:
        both = jnp.where(left, pltpu.roll(high, HEAD_DIM, 1), low)
    return both.astype(BF)


def attend(jobs, slots):
    def scores(job):
        return jnp.dot(job[0](), job[1], preferred_element_type=F32)

    slots[0, : jobs[0][4]] = scores(jobs[0])
    for i, (_, _, values, done, count) in enumerate(jobs):
        if i + 1 < len(jobs):
            slots[(i + 1) % 2, : jobs[i + 1][4]] = scores(jobs[i + 1])
        s = slots[i % 2, :count]
        peak = jnp.max(s, axis=1, keepdims=True)
        weights = jnp.exp2(s - peak).astype(BF)
        done(jnp.dot(weights, values, preferred_element_type=F32), peak)


def near_kernel(q, own, theirs, _, acc_out, peak_out, keys, values, queries, slots):
    rows = q.shape[0]
    block = slots.shape[1]
    for i, kv in enumerate((own, theirs)):
        fill(keys, values, i * rows, kv[:, :LANES], kv[:, LANES:])
    jobs = []
    for head in range(2):
        queries[head] = split_queries(q[...], head)
        for r in range(rows // block):
            at = slice(r * block, (r + 1) * block)

            def done(acc, peak, head=head, at=at):
                acc_out[head, at, :] = acc
                peak_out[head, at, :] = jnp.broadcast_to(peak, acc.shape)

            jobs.append(
                (lambda head=head, at=at: queries[head, at, :], keys[head], values[head], done, block)
            )
    attend(jobs, slots)


def near_attention(q, pair, own, theirs, after):
    rows = q.shape[0]
    block = 256
    return pl.pallas_call(
        near_kernel,
        grid=(1,),
        out_shape=[shape(2, rows, LANES, dtype=F32)] * 2,
        in_specs=[
            pl.BlockSpec((rows, LANES), lambda i: (0, pair)),
            pl.BlockSpec((rows, 2 * LANES), lambda i: (0, 0)),
            pl.BlockSpec((rows, 2 * LANES), lambda i: (0, 0)),
            ANY,
        ],
        out_specs=[pl.BlockSpec((2, rows, LANES), lambda i: (0, 0, 0))] * 2,
        scratch_shapes=[
            pltpu.VMEM((2, LANES, GROUP), BF),
            pltpu.VMEM((2, GROUP, LANES), BF),
            pltpu.VMEM((2, rows, LANES), BF),
            pltpu.VMEM((2, block, GROUP), F32),
        ],
        compiler_params=PARAMS,
        cost_estimate=cost(8 * 10**9, 4 * 10**6),
    )(q, own, theirs, after)


def pair_columns(pair):
    return (
        slice(pair * LANES, (pair + 1) * LANES),
        slice(2 * pair * LANES, (2 * pair + 1) * LANES),
        slice((2 * pair + 1) * LANES, (2 * pair + 2) * LANES),
    )


def middle_kernel(q, *refs):
    pieces, (acc_out, peak_out, keys, values, slots) = refs[:8], refs[8:]
    count = q.shape[0]
    jobs = []
    for pair in range(2):
        lanes, k_at, v_at = pair_columns(pair)
        at = 0
        for piece in pieces:
            fill(keys.at[pair], values.at[pair], at, piece[:, k_at], piece[:, v_at])
            at += piece.shape[0]
        for head in range(2):

            def done(acc, peak, index=2 * pair + head):
                acc_out[index] = acc
                peak_out[index] = jnp.broadcast_to(peak, acc.shape)

            jobs.append(
                (
                    lambda lanes=lanes, head=head: split_queries(q[:, lanes], head),
                    keys[pair, head],
                    values[pair, head],
                    done,
                    count,
                )
            )
    attend(jobs, slots)


def middle_attention(q, pieces):
    count, own = q.shape
    heads = own // HEAD_DIM
    return pl.pallas_call(
        middle_kernel,
        out_shape=[shape(heads, count, LANES, dtype=F32)] * 2,
        in_specs=[VMEM] * 9,
        out_specs=[VMEM] * 2,
        scratch_shapes=[
            pltpu.VMEM((2, 2, LANES, GROUP), BF),
            pltpu.VMEM((2, 2, GROUP, LANES), BF),
            pltpu.VMEM((2, count, GROUP), F32),
        ],
        compiler_params=PARAMS,
        cost_estimate=cost(4 * 10**9, 4 * 10**6),
    )(q, *pieces)


def merge_kernel(me, offsets, qf, *refs):
    pieces, accs_in, peaks_in, mid_acc, mid_peak = (
        refs[:8],
        refs[8:10],
        refs[10:12],
        refs[12],
        refs[13],
    )
    outs, (keys, values, slots, acc, peak, done_rows) = refs[14:18], refs[18:]
    left = left_lanes()
    rows = acc.shape[2]
    few = qf.shape[0]

    def blend(pair, head, which, more, more_peak):
        rate = (MID_RATE, FAR_RATE)[which]
        chosen = pl.ds(offsets[2 * pair + head, which], rows // rate, stride=rate)
        a, p = acc.at[pair, head], peak.at[pair, head]
        old, old_peak = a[chosen, :], p[chosen, :]
        top = jnp.maximum(old_peak, more_peak)
        a[chosen, :] = old * jnp.exp2(old_peak - top) + more * jnp.exp2(more_peak - top)
        p[chosen, :] = top

    jobs = []
    for pair in range(2):
        acc[pair] = accs_in[pair][...]
        peak[pair] = peaks_in[pair][...]
        lanes, k_at, v_at = pair_columns(pair)
        at = 0
        for piece in pieces:
            fill(keys.at[pair], values.at[pair], at, piece[:, k_at], piece[:, v_at])
            at += piece.shape[0]
        for head in range(2):

            def done(more, more_peak, pair=pair, head=head):
                blend(pair, head, 0, mid_acc[2 * pair + head], mid_peak[2 * pair + head])
                blend(pair, head, 1, more, jnp.broadcast_to(more_peak, more.shape))

            jobs.append(
                (
                    lambda lanes=lanes, head=head: split_queries(qf[:, lanes], head),
                    keys[pair, head],
                    values[pair, head],
                    done,
                    few,
                )
            )
    attend(jobs, slots)
    for pair in range(2):
        a, b = acc[pair, 0], acc[pair, 1]
        total = pltpu.roll(jnp.where(left, b, a), HEAD_DIM, 1)
        done_rows[:, pair * LANES : (pair + 1) * LANES] = (jnp.where(left, a, b) / total).astype(BF)
    block = outs[0].shape[0]
    for d, out in enumerate(outs):
        at = pl.multiple_of((me[0] ^ d) * block, block)
        out[...] = done_rows[pl.ds(at, block), :]


def merge(me, offsets, qf, pieces, accs, peaks, mid_acc, mid_peak):
    few, own = qf.shape
    rows = accs[0].shape[1]
    return pl.pallas_call(
        merge_kernel,
        out_shape=[shape(rows // 4, own)] * 4,
        in_specs=[SMEM, SMEM] + [VMEM] * 15,
        out_specs=[VMEM] * 4,
        scratch_shapes=[
            pltpu.VMEM((2, 2, LANES, GROUP), BF),
            pltpu.VMEM((2, 2, GROUP, LANES), BF),
            pltpu.VMEM((2, few, GROUP), F32),
            pltpu.VMEM((2, 2, rows, LANES), F32),
            pltpu.VMEM((2, 2, rows, LANES), F32),
            pltpu.VMEM((rows, own), BF),
        ],
        compiler_params=PARAMS,
        cost_estimate=cost(2 * 10**9, 9 * 10**6),
    )(me, offsets, qf, *pieces, *accs, *peaks, mid_acc, mid_peak)


def out_kernel(me, a0, a1, a2, a3, weight, *outs):
    depth = a0.shape[1]
    for d, out in enumerate(outs):
        columns = pl.ds(pl.multiple_of((me[0] ^ d) * depth, depth), depth)
        total = None
        for e, part in enumerate((a0, a1, a2, a3)):
            rows = pl.ds(pl.multiple_of((me[0] ^ e) * depth, depth), depth)
            term = jnp.dot(part[...], weight[rows, columns], preferred_element_type=F32)
            total = term if total is None else total + term
        out[...] = total.astype(BF)


def project_out(me, parts, weight):
    rows, own = parts[0].shape
    return pl.pallas_call(
        out_kernel,
        out_shape=[shape(rows, own)] * 4,
        in_specs=[SMEM] + [VMEM] * 5,
        out_specs=[VMEM] * 4,
        compiler_params=PARAMS,
        cost_estimate=cost(10**9, 3 * 10**6),
    )(me, *parts, weight)


def place_kernel(me, b0, b1, b2, b3, out):
    block = b0.shape[0]
    for d, part in enumerate((b0, b1, b2, b3)):
        out[pl.ds(pl.multiple_of((me[0] ^ d) * block, block), block), :] = part[...]


def place(me, parts):
    rows, own = parts[0].shape
    return pl.pallas_call(
        place_kernel,
        out_shape=shape(4 * rows, own),
        in_specs=[SMEM] + [VMEM] * 4,
        out_specs=VMEM,
        compiler_params=PARAMS,
    )(me, *parts)


def seg_move(array, target):
    pairs = []
    for i in range(64):
        x, z, core = i // 16, i // 2 % 8, i % 2
        x, z, core = target(x, z, core)
        pairs.append((i, (x % 4 * 8 + z % 8) * 2 + core))
    return lax.ppermute(array, "seg", pairs)


def swap_core(array):
    return seg_move(array, lambda x, z, core: (x, z, 1 - core))


def near_z(array, distance):
    return seg_move(array, lambda x, z, core: (x, z ^ distance, core))


def both_ways(array, distance):
    return seg_move(array, lambda x, z, core: (x, z + (distance if core == 0 else -distance), core))


def along_x(array, distance):
    return seg_move(array, lambda x, z, core: (x ^ distance, z, core))


def swap_head(array, distance):
    return lax.ppermute(array, "head", [(i, i ^ distance) for i in range(4)])


def stack_kernel(*refs, counts):
    out, at = refs[-1], 0
    for ref, count in zip(refs, counts):
        out[at : at + count, :] = ref[:count, :]
        at += count


def stack(parts, after=None):
    counts = tuple(count for _, count in parts)
    extra = [] if after is None else [after]
    return pl.pallas_call(
        functools.partial(stack_kernel, counts=counts),
        out_shape=shape(sum(counts), parts[0][0].shape[1]),
        in_specs=[VMEM] * len(parts) + [ANY] * len(extra),
        out_specs=VMEM,
        compiler_params=PARAMS,
    )(*[array for array, _ in parts], *extra)


def pass_kernel(*refs):
    del refs


def hold(arrays, after):
    count = len(arrays)
    return pl.pallas_call(
        pass_kernel,
        out_shape=[shape(*a.shape, dtype=a.dtype) for a in arrays],
        in_specs=[ANY] * (count + 1),
        out_specs=[ANY] * count,
        input_output_aliases={i: i for i in range(count)},
        compiler_params=PARAMS,
    )(*arrays, after)


def shards(tokens, norm_gain, qkv_weight, out_weight, offsets):
    me = lax.axis_index("head").astype(jnp.int32).reshape(1)
    q, kv0, kv1, qm, kvm, qf, kvf = project(offsets, tokens, norm_gain, qkv_weight)
    far_rows = kvf.shape[0]
    other0, other1 = swap_core(kv0), swap_core(kv1)
    chip = stack([(kvf, far_rows), (swap_core(kvf), far_rows)])
    one, two = both_ways(chip, 1), both_ways(chip, 2)
    onward = stack([(chip, 2 * far_rows), (one, far_rows)])
    three = both_ways(onward, 3)
    mids = [near_z(kvm, distance) for distance in (1, 2, 3)]
    acc0, peak0 = near_attention(q, 0, kv0, other0, onward)
    line = stack(
        [(kvf, far_rows), (one, 2 * far_rows), (two, 2 * far_rows), (three, 3 * far_rows)], acc0
    )
    columns = [along_x(line, distance) for distance in (1, 2, 3)]
    acc1, peak1 = near_attention(q, 1, kv1, other1, line)
    mids = [kvm, *hold(mids, acc1)]
    mids = mids + [swap_core(piece) for piece in mids]
    fars = [line, *hold(columns, acc1)]
    fars = fars + [swap_core(piece) for piece in fars]
    mid_acc, mid_peak = middle_attention(qm, mids)
    parts = merge(me, offsets, qf, fars, (acc0, acc1), (peak0, peak1), mid_acc, mid_peak)
    parts = [parts[0]] + [swap_head(parts[d], d) for d in (1, 2, 3)]
    parts = project_out(me, parts, out_weight)
    parts = [parts[0]] + [swap_head(parts[d], d) for d in (1, 2, 3)]
    return place(me, parts)


def solution(mesh):
    placed = (P("seg", None), P(), P(None, None, "head"), P(), P("head", None))
    return jax.shard_map(
        shards, mesh=mesh, in_specs=placed, out_specs=P("seg", "head"), check_vma=False
    )
```

time: 130 us -> 105 us (0.81)
  waiting for transfers between devices: 42.7 us -> 23.2 us
  starting transfers between devices: 43.8 us -> 33.1 us
  Pallas kernels: 36.4 us -> 42.1 us
    ppermute x21 -> x20, starting transfers between devices: 39.9 us -> 25.3 us  [seg_move(): return lax.ppermute(array, 'seg', pairs)]
    ppermute x3 -> x6, waiting for transfers between devices: 25 us -> 14.9 us  [swap_head(): return lax.ppermute(array, 'head', [(i, i ^ distance) for i in range(4)])]
    ppermute x21 -> x20, waiting for transfers between devices: 17.7 us -> 8.27 us  [seg_move(): return lax.ppermute(array, 'seg', pairs)]
    pallas_call x4 -> x11, Pallas kernels: 31.3 us -> 36.9 us  [the longest x2 15.2 us: near_attention(): pl.pallas_call(near_kernel, grid=(1,), out_shape=[shape(2, rows, LANES, d...]
    ppermute x3 -> x6, starting transfers between devices: 3.92 us -> 7.79 us  [swap_head(): return lax.ppermute(array, 'head', [(i, i ^ distance) for i in range(4)])]
    unnamed x45 -> x57, local copies, waits for them, and re-layouts: 4.72 us -> 6.22 us
  transfers between devices with their start and end apart: 24 -> 26, of which waited for: 7 -> 9; matrix products, arithmetic and copies ran while one was open for 1% -> 0% of each run, Pallas kernels for 14% -> 24%
where the time goes in v2:
time: 105 us
  Pallas kernels  42.1 us (40%)
  starting transfers between devices  33.1 us (32%)
  waiting for transfers between devices  23.2 us (22%)
  local copies, waits for them, and re-layouts  6.22 us (6%)
    ppermute x20, starting transfers between devices, seg_move(): return lax.ppermute(array, 'seg', pairs)  25.3 us
    pallas_call x2, Pallas kernels, near_attention(): pl.pallas_call(near_kernel, grid=(1,), out_shape=[shape(2, rows, LANES, d...  15.2 us
    ppermute x6, waiting for transfers between devices, swap_head(): return lax.ppermute(array, 'head', [(i, i ^ distance) for i in range(4)])  14.9 us
    ppermute x20, waiting for transfers between devices, seg_move(): return lax.ppermute(array, 'seg', pairs)  8.27 us
    ppermute x6, starting transfers between devices, swap_head(): return lax.ppermute(array, 'head', [(i, i ^ distance) for i in range(4)])  7.79 us
    pallas_call x1, Pallas kernels, merge(): pl.pallas_call(merge_kernel, out_shape=[shape(rows // 4, own)] * 4, in_sp...  6.37 us
    unnamed x57, local copies, waits for them, and re-layouts  6.22 us
    pallas_call x1, Pallas kernels, middle_attention(): pl.pallas_call(middle_kernel, out_shape=[shape(heads, count, LANES, dtype...  5.47 us
  transfers between devices with their start and end apart: 26, of which 9 were waited for; matrix products, arithmetic and copies ran while one was open for 0% of the time, Pallas kernels for 24%

profile of v2, /device:TPU:1, one launch (start us, length us, event | category | flops | bytes accessed | tf_op | source)
XLA Modules:
  0.0 104.7 jit_solution(1255503696364888464)
XLA Ops:
  1.3 5.2 %shard_map.55 = (bf16[1024,256]{1,0:T(8,128)(2,1)}, bf16[1024,256]{1,0:T(8,128)(2,1)}, bf16[1024,256]{1,0:T(8,128)(2,1)}, bf16[256,256]{1,0:T(8,128)(2,1)}, bf16...) custom-call(s32[4,2]{1,0:T(4,128)} %copy.13.offsets, bf16[1024,1024]{1,0:T(8,128)(2,1)} %tokens.1, ...), custom_call_target="tpu_custom_call" | custom-call | flops 2000000000 | bytes 6000000 | tf_op jit(solution)/shard_map/pallas_call | solution.py:84
  6.5 3.3 %collective-permute-start.4 = (bf16[1024,256]{1,0:T(8,128)(2,1)}, bf16[1024,256]{1,0:T(8,128)(2,1)S(1)}, u32[]{:S(2)}, u32[]{:S(2)}) collective-permute-start(bf16[1024,256]{1,0:T(8,128)(2,1)} %get-tuple-element.35.own), channel_id=1, source_target_pairs={{0,4},{4,0},{8,12},{12,8},{16,20},{20,16},{24,28},{28,24},{32,36},... | collective-permute-start | bytes 1572872 | tf_op jit(solution)/shard_map/ppermute | solution.py:381
  9.9 1.7 %collective-permute-done.refs_1_ = bf16[32,512]{1,0:T(8,128)(2,1)S(1)} collective-permute-done((bf16[32,512]{1,0:T(8,128)(2,1)}, bf16[32,512]{1,0:T(8,128)(2,1)S(1)}, u32[]{:S(2)}, u32[]{:S(2)}) %collective-permute-start) | collective-permute-done | bytes 32800 | tf_op jit(solution)/shard_map/ppermute | solution.py:381
  13.6 3.8 %collective-permute-start.1 = (bf16[64,512]{1,0:T(8,128)(2,1)}, bf16[64,512]{1,0:T(8,128)(2,1)S(1)}, u32[]{:S(2)}, u32[]{:S(2)}) collective-permute-start(bf16[64,512]{1,0:T(8,128)(2,1)} %shard_map.56.refs_0_), channel_id=1, source_target_pairs={{0,8},{4,60},{8,16},{12,4},{16,24},{20,12},{24,32},{28,20},{32,40}... | collective-permute-start | bytes 196616 | tf_op jit(solution)/shard_map/ppermute | solution.py:381
  17.4 3.1 %collective-permute-start.8 = (bf16[1024,256]{1,0:T(8,128)(2,1)}, bf16[1024,256]{1,0:T(8,128)(2,1)S(1)}, u32[]{:S(2)}, u32[]{:S(2)}) collective-permute-start(bf16[1024,256]{1,0:T(8,128)(2,1)} %get-tuple-element.37.own), channel_id=1, source_target_pairs={{0,4},{4,0},{8,12},{12,8},{16,20},{20,16},{24,28},{28,24},{32,36},... | collective-permute-start | bytes 1572872 | tf_op jit(solution)/shard_map/ppermute | solution.py:381
  23.3 1.7 %collective-permute-start.3 = (bf16[96,512]{1,0:T(8,128)(2,1)}, bf16[96,512]{1,0:T(8,128)(2,1)S(1)}, u32[]{:S(2)}, u32[]{:S(2)}) collective-permute-start(bf16[96,512]{1,0:T(8,128)(2,1)} %shard_map.57._), channel_id=1, source_target_pairs={{0,24},{4,44},{8,32},{12,52},{16,40},{20,60},{24,48},{28,4},{32,56... | collective-permute-start | bytes 294920 | tf_op jit(solution)/shard_map/ppermute | solution.py:381
  25.0 7.6 %shard_map.58 = (f32[2,1024,128]{2,1,0:T(8,128)}, f32[2,1024,128]{2,1,0:T(8,128)}) custom-call(bf16[1024,256]{1,0:T(8,128)(2,1)} %get-tuple-element.34.q, bf16[1024,256]{1,0:T(8,128)(2,1)} %get-tuple-element.35.own, bf16[1024,256]{1,0:T(8,128)(2,1)} %copy-done.15, bf16[96,512]{1,0:T(8,128)(2,1)} %shard_map.57._), custom_call_target="tpu_custom_call" | custom-call | flops 8000000000 | bytes 4000000 | tf_op jit(solution)/shard_map/pallas_call | solution.py:180
  32.6 3.3 %collective-permute-done.2.refs_2_ = bf16[64,512]{1,0:T(8,128)(2,1)S(1)} collective-permute-done((bf16[64,512]{1,0:T(8,128)(2,1)}, bf16[64,512]{1,0:T(8,128)(2,1)S(1)}, u32[]{:S(2)}, u32[]{:S(2)}) %collective-permute-start.2) | collective-permute-done | bytes 65568 | tf_op jit(solution)/shard_map/ppermute | solution.py:381
  36.7 1.7 %shard_map.59._.refs_0_ = bf16[256,512]{1,0:T(8,128)(2,1)} custom-call(bf16[32,512]{1,0:T(8,128)(2,1)} %get-tuple-element.33.refs_0_, bf16[64,512]{1,0:T(8,128)(2,1)} %copy-done.6, bf16[64,512]{1,0:T(8,128)(2,1)} %copy-done.12, bf16[96,512]{1,0:T(8,128)(2,1)} %copy-done.11, f32[2,1024,128]{2,1,0:T(8,128)} %get-tuple-element.36.refs_4_.refs_8_), custom_call_target="tpu_custom_call" | custom-call | tf_op jit(solution)/shard_map/pallas_call | solution.py:414
  39.6 2.5 %collective-permute-start.6 = (bf16[256,512]{1,0:T(8,128)(2,1)}, bf16[256,512]{1,0:T(8,128)(2,1)S(1)}, u32[]{:S(2)}, u32[]{:S(2)}) collective-permute-start(bf16[256,512]{1,0:T(8,128)(2,1)} %shard_map.59._.refs_0_), channel_id=1, source_target_pairs={{0,128},{4,132},{8,136},{12,140},{16,144},{20,148},{24,152},{28,15... | collective-permute-start | bytes 786440 | tf_op jit(solution)/shard_map/ppermute | solution.py:381
  42.0 7.6 %shard_map.60 = (f32[2,1024,128]{2,1,0:T(8,128)}, f32[2,1024,128]{2,1,0:T(8,128)}) custom-call(bf16[1024,256]{1,0:T(8,128)(2,1)} %get-tuple-element.34.q, bf16[1024,256]{1,0:T(8,128)(2,1)} %get-tuple-element.37.own, bf16[1024,256]{1,0:T(8,128)(2,1)} %copy-done.14, bf16[256,512]{1,0:T(8,128)(2,1)} %shard_map.59._.refs_0_), custom_call_target="tpu_custom_call" | custom-call | flops 8000000000 | bytes 4000000 | tf_op jit(solution)/shard_map/pallas_call | solution.py:180
  49.9 2.8 %collective-permute-start.16 = (bf16[256,512]{1,0:T(8,128)(2,1)S(1)}, bf16[256,512]{1,0:T(8,128)(2,1)S(1)}, u32[]{:S(2)}, u32[]{:S(2)}) collective-permute-start(bf16[256,512]{1,0:T(8,128)(2,1)S(1)} %copy-done.16), channel_id=1, source_target_pairs={{0,4},{4,0},{8,12},{12,8},{16,20},{20,16},{24,28},{28,24},{32,36},... | collective-permute-start | bytes 786440 | tf_op jit(solution)/shard_map/ppermute | solution.py:381
  55.2 3.2 %collective-permute-done.7.refs_2_ = bf16[256,512]{1,0:T(8,128)(2,1)S(1)} collective-permute-done((bf16[256,512]{1,0:T(8,128)(2,1)S(1)}, bf16[256,512]{1,0:T(8,128)(2,1)S(1)}, u32[]{:S(2)}, u32[]{:S(2)}) %collective-permute-start.7) | collective-permute-done | bytes 262176 | tf_op jit(solution)/shard_map/ppermute | solution.py:381
  58.4 2.3 %collective-permute-start.9 = (bf16[256,512]{1,0:T(8,128)(2,1)S(1)}, bf16[256,512]{1,0:T(8,128)(2,1)S(1)}, u32[]{:S(2)}, u32[]{:S(2)}) collective-permute-start(bf16[256,512]{1,0:T(8,128)(2,1)S(1)} %copy-done.7), channel_id=1, source_target_pairs={{0,4},{4,0},{8,12},{12,8},{16,20},{20,16},{24,28},{28,24},{32,36},... | collective-permute-start | bytes 786440 | tf_op jit(solution)/shard_map/ppermute | solution.py:381
  62.7 5.5 %shard_map.63 = (f32[4,256,128]{2,1,0:T(8,128)}, f32[4,256,128]{2,1,0:T(8,128)}) custom-call(bf16[256,256]{1,0:T(8,128)(2,1)} %get-tuple-element.44.q, bf16[256,512]{1,0:T(8,128)(2,1)} %get-tuple-element.45.refs_0_, bf16[256,512]{1,0:T(8,128)(2,1)} %get-tuple-element.46.refs_1_, bf16[256,512]{1,0:T(8,128)(2,1)} %get-tuple-element.47.refs_2_, ...), custom_call_target="tpu_custom_call" | custom-call | flops 4000000000 | bytes 4000000 | tf_op jit(solution)/shard_map/pallas_call | solution.py:241
  69.1 6.4 %shard_map.64 = (bf16[256,256]{1,0:T(8,128)(2,1)}, bf16[256,256]{1,0:T(8,128)(2,1)}, bf16[256,256]{1,0:T(8,128)(2,1)}, bf16[256,256]{1,0:T(8,128)(2,1)}) custom-call(s32[1]{0:T(128)} %bitcast.me, s32[4,2]{1,0:T(4,128)} %copy.13.offsets, bf16[32,256]{1,0:T(8,128)(2,1)} %get-tuple-element.32.qf, bf16[256,512]{1,0:T(8,128)(2,1)} %shard_map.59._.refs_0_, ...), custom_call_target="tpu_custom_call" | custom-call | flops 2000000000 | bytes 9000000 | tf_op jit(solution)/shard_map/pallas_call | solution.py:316
  76.8 2.6 %collective-permute-start.21 = (bf16[256,256]{1,0:T(8,128)(2,1)}, bf16[256,256]{1,0:T(8,128)(2,1)S(1)}, u32[]{:S(2)}, u32[]{:S(2)}) collective-permute-start(bf16[256,256]{1,0:T(8,128)(2,1)} %get-tuple-element.53), channel_id=1, source_target_pairs={{0,2},{1,3},{2,0},{3,1},{4,6},{5,7},{6,4},{7,5},{8,10},{9,11},{10,... | collective-permute-start | bytes 393224 | tf_op jit(solution)/shard_map/ppermute | solution.py:401
  80.5 5.3 %collective-permute-done.21.a2 = bf16[256,256]{1,0:T(8,128)(2,1)S(1)} collective-permute-done((bf16[256,256]{1,0:T(8,128)(2,1)}, bf16[256,256]{1,0:T(8,128)(2,1)S(1)}, u32[]{:S(2)}, u32[]{:S(2)}) %collective-permute-start.21) | collective-permute-done | bytes 131104 | tf_op jit(solution)/shard_map/ppermute | solution.py:401
  85.8 2.5 %collective-permute-done.22.a3 = bf16[256,256]{1,0:T(8,128)(2,1)S(1)} collective-permute-done((bf16[256,256]{1,0:T(8,128)(2,1)}, bf16[256,256]{1,0:T(8,128)(2,1)S(1)}, u32[]{:S(2)}, u32[]{:S(2)}) %collective-permute-start.22) | collective-permute-done | bytes 131104 | tf_op jit(solution)/shard_map/ppermute | solution.py:401
  88.9 3.3 %shard_map.65 = (bf16[256,256]{1,0:T(8,128)(2,1)}, bf16[256,256]{1,0:T(8,128)(2,1)}, bf16[256,256]{1,0:T(8,128)(2,1)}, bf16[256,256]{1,0:T(8,128)(2,1)}) custom-call(s32[1]{0:T(128)} %bitcast.me, bf16[256,256]{1,0:T(8,128)(2,1)} %get-tuple-element.51.a0, bf16[256,256]{1,0:T(8,128)(2,1)} %copy-done.25, bf16[256,256]{1,0:T(8,128)(2,1)} %copy-done.26, ...), custom_call_target="tpu_custom_call" | custom-call | flops 1000000000 | bytes 3000000 | tf_op jit(solution)/shard_map/pallas_call | solution.py:348
  93.8 2.3 %collective-permute-start.25 = (bf16[256,256]{1,0:T(8,128)(2,1)}, bf16[256,256]{1,0:T(8,128)(2,1)S(1)}, u32[]{:S(2)}, u32[]{:S(2)}) collective-permute-start(bf16[256,256]{1,0:T(8,128)(2,1)} %get-tuple-element.58), channel_id=1, source_target_pairs={{0,3},{1,2},{2,1},{3,0},{4,7},{5,6},{6,5},{7,4},{8,11},{9,10},{10,... | collective-permute-start | bytes 393224 | tf_op jit(solution)/shard_map/ppermute | solution.py:401
  96.3 3.4 %collective-permute-done.24.b2 = bf16[256,256]{1,0:T(8,128)(2,1)S(1)} collective-permute-done((bf16[256,256]{1,0:T(8,128)(2,1)}, bf16[256,256]{1,0:T(8,128)(2,1)S(1)}, u32[]{:S(2)}, u32[]{:S(2)}) %collective-permute-start.24) | collective-permute-done | bytes 131104 | tf_op jit(solution)/shard_map/ppermute | solution.py:401
  99.7 2.5 %collective-permute-done.25.b3 = bf16[256,256]{1,0:T(8,128)(2,1)S(1)} collective-permute-done((bf16[256,256]{1,0:T(8,128)(2,1)}, bf16[256,256]{1,0:T(8,128)(2,1)S(1)}, u32[]{:S(2)}, u32[]{:S(2)}) %collective-permute-start.25) | collective-permute-done | bytes 131104 | tf_op jit(solution)/shard_map/ppermute | solution.py:401
  102.8 1.9 %shard_map.66 = bf16[1024,256]{1,0:T(8,128)(2,1)} custom-call(s32[1]{0:T(128)} %bitcast.me, bf16[256,256]{1,0:T(8,128)(2,1)} %get-tuple-element.55.b0, bf16[256,256]{1,0:T(8,128)(2,1)} %copy-done.8, bf16[256,256]{1,0:T(8,128)(2,1)} %copy-done.9, bf16[256,256]{1,0:T(8,128)(2,1)} %copy-done.10), custom_call_target="tpu_custom_call" | custom-call | tf_op jit(solution)/shard_map/pallas_call | solution.py:366
  (97 shorter events, 19.0 us)
Async XLA Ops:
  6.5 16.8 %collective-permute-start.4 = (bf16[1024,256]{1,0:T(8,128)(2,1)}, bf16[1024,256]{1,0:T(8,128)(2,1)S(1)}, u32[]{:S(2)}, u32[]{:S(2)}) collective-permute-start(bf16[1024,256]{1,0:T(8,128)(2,1)} %get-tuple-element.35.own), channel_id=1, source_target_pairs={{0,4},{4,0},{8,12},{12,8},{16,20},{20,16},{24,28},{28,24},{32,36},... | collective-permute-start | bytes 1572872 | tf_op jit(solution)/shard_map/ppermute | solution.py:381
  13.6 7.0 %collective-permute-start.1 = (bf16[64,512]{1,0:T(8,128)(2,1)}, bf16[64,512]{1,0:T(8,128)(2,1)S(1)}, u32[]{:S(2)}, u32[]{:S(2)}) collective-permute-start(bf16[64,512]{1,0:T(8,128)(2,1)} %shard_map.56.refs_0_), channel_id=1, source_target_pairs={{0,8},{4,60},{8,16},{12,4},{16,24},{20,12},{24,32},{28,20},{32,40}... | collective-permute-start | bytes 196616 | tf_op jit(solution)/shard_map/ppermute | solution.py:381
  17.4 32.2 %collective-permute-start.13 = (bf16[256,512]{1,0:T(8,128)(2,1)}, bf16[256,512]{1,0:T(8,128)(2,1)S(1)}, u32[]{:S(2)}, u32[]{:S(2)}) collective-permute-start(bf16[256,512]{1,0:T(8,128)(2,1)} %get-tuple-element.45.refs_0_), channel_id=1, source_target_pairs={{0,8},{4,12},{8,0},{12,4},{16,24},{20,28},{24,16},{28,20},{32,40},... | collective-permute-start | bytes 786440 | tf_op jit(solution)/shard_map/ppermute | solution.py:381
  17.4 32.5 %collective-permute-start.14 = (bf16[256,512]{1,0:T(8,128)(2,1)}, bf16[256,512]{1,0:T(8,128)(2,1)S(1)}, u32[]{:S(2)}, u32[]{:S(2)}) collective-permute-start(bf16[256,512]{1,0:T(8,128)(2,1)} %get-tuple-element.45.refs_0_), channel_id=1, source_target_pairs={{0,16},{4,20},{8,24},{12,28},{16,0},{20,4},{24,8},{28,12},{32,48},... | collective-permute-start | bytes 786440 | tf_op jit(solution)/shard_map/ppermute | solution.py:381
  17.4 22.1 %collective-permute-start.8 = (bf16[1024,256]{1,0:T(8,128)(2,1)}, bf16[1024,256]{1,0:T(8,128)(2,1)S(1)}, u32[]{:S(2)}, u32[]{:S(2)}) collective-permute-start(bf16[1024,256]{1,0:T(8,128)(2,1)} %get-tuple-element.37.own), channel_id=1, source_target_pairs={{0,4},{4,0},{8,12},{12,8},{16,20},{20,16},{24,28},{28,24},{32,36},... | collective-permute-start | bytes 1572872 | tf_op jit(solution)/shard_map/ppermute | solution.py:381
  20.6 15.4 %collective-permute-start.2 = (bf16[64,512]{1,0:T(8,128)(2,1)}, bf16[64,512]{1,0:T(8,128)(2,1)S(1)}, u32[]{:S(2)}, u32[]{:S(2)}) collective-permute-start(bf16[64,512]{1,0:T(8,128)(2,1)} %shard_map.56.refs_0_), channel_id=1, source_target_pairs={{0,16},{4,52},{8,24},{12,60},{16,32},{20,4},{24,40},{28,12},{32,48... | collective-permute-start | bytes 196616 | tf_op jit(solution)/shard_map/ppermute | solution.py:381
  23.3 12.7 %collective-permute-start.3 = (bf16[96,512]{1,0:T(8,128)(2,1)}, bf16[96,512]{1,0:T(8,128)(2,1)S(1)}, u32[]{:S(2)}, u32[]{:S(2)}) collective-permute-start(bf16[96,512]{1,0:T(8,128)(2,1)} %shard_map.57._), channel_id=1, source_target_pairs={{0,24},{4,44},{8,32},{12,52},{16,40},{20,60},{24,48},{28,4},{32,56... | collective-permute-start | bytes 294920 | tf_op jit(solution)/shard_map/ppermute | solution.py:381
  36.0 16.7 %collective-permute-start.15 = (bf16[256,512]{1,0:T(8,128)(2,1)S(1)}, bf16[256,512]{1,0:T(8,128)(2,1)S(1)}, u32[]{:S(2)}, u32[]{:S(2)}) collective-permute-start(bf16[256,512]{1,0:T(8,128)(2,1)S(1)} %copy-done.16), channel_id=1, source_target_pairs={{0,24},{4,28},{8,16},{12,20},{16,8},{20,12},{24,0},{28,4},{32,56},... | collective-permute-start | bytes 786440 | tf_op jit(solution)/shard_map/ppermute | solution.py:381
  38.4 15.2 %collective-permute-start.5 = (bf16[256,512]{1,0:T(8,128)(2,1)}, bf16[256,512]{1,0:T(8,128)(2,1)S(1)}, u32[]{:S(2)}, u32[]{:S(2)}) collective-permute-start(bf16[256,512]{1,0:T(8,128)(2,1)} %shard_map.59._.refs_0_), channel_id=1, source_target_pairs={{0,64},{4,68},{8,72},{12,76},{16,80},{20,84},{24,88},{28,92},{32,9... | collective-permute-start | bytes 786440 | tf_op jit(solution)/shard_map/ppermute | solution.py:381
  39.6 14.3 %collective-permute-start.6 = (bf16[256,512]{1,0:T(8,128)(2,1)}, bf16[256,512]{1,0:T(8,128)(2,1)S(1)}, u32[]{:S(2)}, u32[]{:S(2)}) collective-permute-start(bf16[256,512]{1,0:T(8,128)(2,1)} %shard_map.59._.refs_0_), channel_id=1, source_target_pairs={{0,128},{4,132},{8,136},{12,140},{16,144},{20,148},{24,152},{28,15... | collective-permute-start | bytes 786440 | tf_op jit(solution)/shard_map/ppermute | solution.py:381
  49.6 8.8 %collective-permute-start.7 = (bf16[256,512]{1,0:T(8,128)(2,1)S(1)}, bf16[256,512]{1,0:T(8,128)(2,1)S(1)}, u32[]{:S(2)}, u32[]{:S(2)}) collective-permute-start(bf16[256,512]{1,0:T(8,128)(2,1)S(1)} %copy-done.7), channel_id=1, source_target_pairs={{0,192},{4,196},{8,200},{12,204},{16,208},{20,212},{24,216},{28,22... | collective-permute-start | bytes 786440 | tf_op jit(solution)/shard_map/ppermute | solution.py:381
  49.9 10.8 %collective-permute-start.16 = (bf16[256,512]{1,0:T(8,128)(2,1)S(1)}, bf16[256,512]{1,0:T(8,128)(2,1)S(1)}, u32[]{:S(2)}, u32[]{:S(2)}) collective-permute-start(bf16[256,512]{1,0:T(8,128)(2,1)S(1)} %copy-done.16), channel_id=1, source_target_pairs={{0,4},{4,0},{8,12},{12,8},{16,20},{20,16},{24,28},{28,24},{32,36},... | collective-permute-start | bytes 786440 | tf_op jit(solution)/shard_map/ppermute | solution.py:381
  53.4 8.0 %collective-permute-start.17 = (bf16[256,512]{1,0:T(8,128)(2,1)}, bf16[256,512]{1,0:T(8,128)(2,1)S(1)}, u32[]{:S(2)}, u32[]{:S(2)}) collective-permute-start(bf16[256,512]{1,0:T(8,128)(2,1)} %get-tuple-element.46.refs_1_), channel_id=1, source_target_pairs={{0,4},{4,0},{8,12},{12,8},{16,20},{20,16},{24,28},{28,24},{32,36},... | collective-permute-start | bytes 786440 | tf_op jit(solution)/shard_map/ppermute | solution.py:381
  53.5 8.0 %collective-permute-start.18 = (bf16[256,512]{1,0:T(8,128)(2,1)}, bf16[256,512]{1,0:T(8,128)(2,1)S(1)}, u32[]{:S(2)}, u32[]{:S(2)}) collective-permute-start(bf16[256,512]{1,0:T(8,128)(2,1)} %get-tuple-element.47.refs_2_), channel_id=1, source_target_pairs={{0,4},{4,0},{8,12},{12,8},{16,20},{20,16},{24,28},{28,24},{32,36},... | collective-permute-start | bytes 786440 | tf_op jit(solution)/shard_map/ppermute | solution.py:381
  53.9 8.0 %collective-permute-start.19 = (bf16[256,512]{1,0:T(8,128)(2,1)}, bf16[256,512]{1,0:T(8,128)(2,1)S(1)}, u32[]{:S(2)}, u32[]{:S(2)}) collective-permute-start(bf16[256,512]{1,0:T(8,128)(2,1)} %get-tuple-element.48.refs_3_), channel_id=1, source_target_pairs={{0,4},{4,0},{8,12},{12,8},{16,20},{20,16},{24,28},{28,24},{32,36},... | collective-permute-start | bytes 786440 | tf_op jit(solution)/shard_map/ppermute | solution.py:381
  58.4 9.7 %collective-permute-start.9 = (bf16[256,512]{1,0:T(8,128)(2,1)S(1)}, bf16[256,512]{1,0:T(8,128)(2,1)S(1)}, u32[]{:S(2)}, u32[]{:S(2)}) collective-permute-start(bf16[256,512]{1,0:T(8,128)(2,1)S(1)} %copy-done.7), channel_id=1, source_target_pairs={{0,4},{4,0},{8,12},{12,8},{16,20},{20,16},{24,28},{28,24},{32,36},... | collective-permute-start | bytes 786440 | tf_op jit(solution)/shard_map/ppermute | solution.py:381
  60.8 7.4 %collective-permute-start.10 = (bf16[256,512]{1,0:T(8,128)(2,1)}, bf16[256,512]{1,0:T(8,128)(2,1)S(1)}, u32[]{:S(2)}, u32[]{:S(2)}) collective-permute-start(bf16[256,512]{1,0:T(8,128)(2,1)} %get-tuple-element.39.refs_1_), channel_id=1, source_target_pairs={{0,4},{4,0},{8,12},{12,8},{16,20},{20,16},{24,28},{28,24},{32,36},... | collective-permute-start | bytes 786440 | tf_op jit(solution)/shard_map/ppermute | solution.py:381
  61.4 6.7 %collective-permute-start.11 = (bf16[256,512]{1,0:T(8,128)(2,1)}, bf16[256,512]{1,0:T(8,128)(2,1)S(1)}, u32[]{:S(2)}, u32[]{:S(2)}) collective-permute-start(bf16[256,512]{1,0:T(8,128)(2,1)} %get-tuple-element.40.refs_2_), channel_id=1, source_target_pairs={{0,4},{4,0},{8,12},{12,8},{16,20},{20,16},{24,28},{28,24},{32,36},... | collective-permute-start | bytes 786440 | tf_op jit(solution)/shard_map/ppermute | solution.py:381
  61.5 6.6 %collective-permute-start.12 = (bf16[256,512]{1,0:T(8,128)(2,1)}, bf16[256,512]{1,0:T(8,128)(2,1)S(1)}, u32[]{:S(2)}, u32[]{:S(2)}) collective-permute-start(bf16[256,512]{1,0:T(8,128)(2,1)} %get-tuple-element.41.refs_3_), channel_id=1, source_target_pairs={{0,4},{4,0},{8,12},{12,8},{16,20},{20,16},{24,28},{28,24},{32,36},... | collective-permute-start | bytes 786440 | tf_op jit(solution)/shard_map/ppermute | solution.py:381
  75.5 5.0 %collective-permute-start.20 = (bf16[256,256]{1,0:T(8,128)(2,1)}, bf16[256,256]{1,0:T(8,128)(2,1)S(1)}, u32[]{:S(2)}, u32[]{:S(2)}) collective-permute-start(bf16[256,256]{1,0:T(8,128)(2,1)} %get-tuple-element.52), channel_id=1, source_target_pairs={{0,1},{1,0},{2,3},{3,2},{4,5},{5,4},{6,7},{7,6},{8,9},{9,8},{10,11... | collective-permute-start | bytes 393224 | tf_op jit(solution)/shard_map/ppermute | solution.py:401
  76.8 9.0 %collective-permute-start.21 = (bf16[256,256]{1,0:T(8,128)(2,1)}, bf16[256,256]{1,0:T(8,128)(2,1)S(1)}, u32[]{:S(2)}, u32[]{:S(2)}) collective-permute-start(bf16[256,256]{1,0:T(8,128)(2,1)} %get-tuple-element.53), channel_id=1, source_target_pairs={{0,2},{1,3},{2,0},{3,1},{4,6},{5,7},{6,4},{7,5},{8,10},{9,11},{10,... | collective-permute-start | bytes 393224 | tf_op jit(solution)/shard_map/ppermute | solution.py:401
  79.4 8.8 %collective-permute-start.22 = (bf16[256,256]{1,0:T(8,128)(2,1)}, bf16[256,256]{1,0:T(8,128)(2,1)S(1)}, u32[]{:S(2)}, u32[]{:S(2)}) collective-permute-start(bf16[256,256]{1,0:T(8,128)(2,1)} %get-tuple-element.54), channel_id=1, source_target_pairs={{0,3},{1,2},{2,1},{3,0},{4,7},{5,6},{6,5},{7,4},{8,11},{9,10},{10,... | collective-permute-start | bytes 393224 | tf_op jit(solution)/shard_map/ppermute | solution.py:401
  92.2 7.4 %collective-permute-start.24 = (bf16[256,256]{1,0:T(8,128)(2,1)}, bf16[256,256]{1,0:T(8,128)(2,1)S(1)}, u32[]{:S(2)}, u32[]{:S(2)}) collective-permute-start(bf16[256,256]{1,0:T(8,128)(2,1)} %get-tuple-element.57), channel_id=1, source_target_pairs={{0,2},{1,3},{2,0},{3,1},{4,6},{5,7},{6,4},{7,5},{8,10},{9,11},{10,... | collective-permute-start | bytes 393224 | tf_op jit(solution)/shard_map/ppermute | solution.py:401
  93.8 8.4 %collective-permute-start.25 = (bf16[256,256]{1,0:T(8,128)(2,1)}, bf16[256,256]{1,0:T(8,128)(2,1)S(1)}, u32[]{:S(2)}, u32[]{:S(2)}) collective-permute-start(bf16[256,256]{1,0:T(8,128)(2,1)} %get-tuple-element.58), channel_id=1, source_target_pairs={{0,3},{1,2},{2,1},{3,0},{4,7},{5,6},{6,5},{7,4},{8,11},{9,10},{10,... | collective-permute-start | bytes 393224 | tf_op jit(solution)/shard_map/ppermute | solution.py:401
  (30 other events, 84.9 us)

commit v3 on v2

v3 whole, which is shorter than its diff:
```python
import functools

import jax
import jax.numpy as jnp
from jax import lax
from jax.experimental import pallas as pl
from jax.experimental.pallas import tpu as pltpu
from jax.sharding import PartitionSpec as P

HEAD_DIM = 64
MID_RATE = 4
FAR_RATE = 32
GROUP = 2048
EPS = 1e-06
LANES = 128
BF = jnp.bfloat16
F32 = jnp.float32
SCALE = 1.4426950408889634 * HEAD_DIM ** (-0.5)
VMEM = pl.BlockSpec(memory_space=pltpu.VMEM)
SMEM = pl.BlockSpec(memory_space=pltpu.SMEM)
ANY = pl.BlockSpec(memory_space=pl.ANY)
PARAMS = pltpu.CompilerParams(vmem_limit_bytes=56 * 2**20)


def shape(*dims, dtype=BF):
    return jax.ShapeDtypeStruct(dims, dtype)


def left_lanes():
    return lax.broadcasted_iota(jnp.int32, (1, LANES), 1) < HEAD_DIM


def cost(flops, bytes_accessed):
    return pl.CostEstimate(flops=flops, bytes_accessed=bytes_accessed, transcendentals=0)


def offset_of(offsets, head, which):
    return jnp.max(offsets[head : head + 1, which : which + 1])


def project_kernel(offsets, tokens, gain, weight, q_out, kv_out, qm_out, kvm_out, qf_out, kvf_out, held):
    rows = tokens.shape[0]
    x = tokens[...].astype(F32)
    mean_square = jnp.mean(x * x, axis=1, keepdims=True)
    normed = (x * lax.rsqrt(mean_square + EPS) * gain[...].astype(F32)[None, :]).astype(BF)
    for part in range(3):
        y = jnp.dot(normed, weight[part], preferred_element_type=F32)
        yb = y.astype(BF)
        if part == 0:
            q_out[...] = yb
        for pair in range(2):
            lanes = slice(pair * LANES, (pair + 1) * LANES)
            held[2 * part + pair] = y[:, lanes]
            if part > 0:
                c = (2 * pair + part - 1) * LANES
                kv_out[:, c : c + LANES] = yb[:, lanes]
    left = left_lanes()
    for rate, which, q_to, kv_to in ((MID_RATE, 0, qm_out, kvm_out), (FAR_RATE, 1, qf_out, kvf_out)):
        count = rows // rate
        for pair in range(2):
            o0 = offset_of(offsets, 2 * pair, which)
            o1 = offset_of(offsets, 2 * pair + 1, which)
            for part in range(3):
                source = held.at[2 * part + pair]
                a = source[pl.ds(o0, count, stride=rate), :]
                b = source[pl.ds(o1, count, stride=rate), :]
                picked = jnp.where(left, a, b).astype(BF)
                if part == 0:
                    q_to[:, pair * LANES : (pair + 1) * LANES] = picked
                else:
                    c = (2 * pair + part - 1) * LANES
                    kv_to[:, c : c + LANES] = picked


def project(offsets, tokens, gain, weight):
    rows, width = tokens.shape
    own = weight.shape[2]
    block = 512

    def rowed(count, columns):
        return pl.BlockSpec((count, columns), lambda i: (i, 0))

    mid, far = block // MID_RATE, block // FAR_RATE
    return pl.pallas_call(
        project_kernel,
        grid=(rows // block,),
        out_shape=[
            shape(rows, own),
            shape(rows, 2 * own),
            shape(rows // MID_RATE, own),
            shape(rows // MID_RATE, 2 * own),
            shape(rows // FAR_RATE, own),
            shape(rows // FAR_RATE, 2 * own),
        ],
        in_specs=[
            pl.BlockSpec(offsets.shape, lambda i: (0, 0)),
            rowed(block, width),
            pl.BlockSpec((width,), lambda i: (0,)),
            pl.BlockSpec((3, width, own), lambda i: (0, 0, 0)),
        ],
        out_specs=[
            rowed(block, own),
            rowed(block, 2 * own),
            rowed(mid, own),
            rowed(mid, 2 * own),
            rowed(far, own),
            rowed(far, 2 * own),
        ],
        scratch_shapes=[pltpu.VMEM((6, block, LANES), F32)],
        compiler_params=PARAMS,
        cost_estimate=cost(2 * 10**9, 6 * 10**6),
    )(offsets, tokens, gain, weight)


def fill(keys, values, at, key_rows, value_rows):
    left = left_lanes()
    count = key_rows.shape[0]
    one = jnp.ones_like(value_rows)
    turned = key_rows.T
    for head in range(2):
        half = turned[head * HEAD_DIM : (head + 1) * HEAD_DIM]
        keys[head, :HEAD_DIM, at : at + count] = half
        keys[head, HEAD_DIM:, at : at + count] = half
    values[0, at : at + count, :] = jnp.where(left, value_rows, one)
    values[1, at : at + count, :] = jnp.where(left, one, value_rows)


def split_queries(q, head):
    left = left_lanes()
    scaled = q.astype(F32) * SCALE
    high = scaled.astype(BF).astype(F32)
    low = scaled - high
    if head == 0:
        both = jnp.where(left, high, pltpu.roll(low, HEAD_DIM, 1))
    else:
        both = jnp.where(left, pltpu.roll(high, HEAD_DIM, 1), low)
    return both.astype(BF)


def attend(jobs, slots):
    def scores(job):
        return jnp.dot(job[0](), job[1], preferred_element_type=F32)

    slots[0, : jobs[0][4]] = scores(jobs[0])
    for i, (_, _, values, done, count) in enumerate(jobs):
        if i + 1 < len(jobs):
            slots[(i + 1) % 2, : jobs[i + 1][4]] = scores(jobs[i + 1])
        s = slots[i % 2, :count]
        peak = jnp.max(s, axis=1, keepdims=True)
        weights = jnp.exp2(s - peak).astype(BF)
        done(jnp.dot(weights, values, preferred_element_type=F32), peak)


def normalised(a, b):
    left = left_lanes()
    total = pltpu.roll(jnp.where(left, b, a), HEAD_DIM, 1)
    return (jnp.where(left, a, b) / total).astype(BF)


def near_kernel(offsets, q, own, theirs, *refs, pair):
    before = refs[0] if pair else None
    refs = refs[1 + pair :]
    out, mid_acc, mid_peak, far_acc, far_peak, acc, peak, keys, values, queries, slots = refs
    rows = q.shape[0]
    block = slots.shape[1]
    for i, kv in enumerate((own, theirs)):
        fill(keys, values, i * rows, kv[:, :LANES], kv[:, LANES:])
    jobs = []
    for head in range(2):
        queries[head] = split_queries(q[...], head)
        for r in range(rows // block):
            at = slice(r * block, (r + 1) * block)

            def done(more, more_peak, head=head, at=at):
                acc[head, at, :] = more
                peak[head, at, :] = jnp.broadcast_to(more_peak, more.shape)

            jobs.append(
                (lambda head=head, at=at: queries[head, at, :], keys[head], values[head], done, block)
            )
    attend(jobs, slots)
    result = normalised(acc[0], acc[1])
    if pair:
        out[:rows, :LANES] = before[...]
        out[:rows, LANES:] = result
        heads = offsets.shape[0]
        row = lax.broadcasted_iota(jnp.int32, (out.shape[0] - rows, out.shape[1]), 0)
        told = jnp.zeros(row.shape, F32)
        for head in range(heads):
            for which in range(2):
                value = offset_of(offsets, head, which).astype(F32)
                told = jnp.where(row == 2 * head + which, value, told)
        out[rows:, :] = told.astype(BF)
    else:
        out[...] = result
    for head in range(2):
        for rate, which, acc_to, peak_to in (
            (MID_RATE, 0, mid_acc, mid_peak),
            (FAR_RATE, 1, far_acc, far_peak),
        ):
            o = offset_of(offsets, 2 * pair + head, which)
            chosen = pl.ds(o, rows // rate, stride=rate)
            acc_to[head] = acc.at[head][chosen, :]
            peak_to[head] = peak.at[head][chosen, :]


def near_attention(offsets, q, pair, own, theirs, after, before=None):
    rows, width = q.shape
    block = 256
    mid, far = rows // MID_RATE, rows // FAR_RATE
    first = shape(rows + 16, width) if pair else shape(rows, LANES)

    def whole(s):
        return pl.BlockSpec(s.shape, lambda i: (0,) * len(s.shape))

    outs = [first] + [shape(2, count, LANES, dtype=F32) for count in (mid, mid, far, far)]
    extra = [before, after] if pair else [after]
    return pl.pallas_call(
        functools.partial(near_kernel, pair=pair),
        grid=(1,),
        out_shape=outs,
        in_specs=[
            whole(offsets),
            pl.BlockSpec((rows, LANES), lambda i: (0, pair)),
            pl.BlockSpec((rows, 2 * LANES), lambda i: (0, pair)),
            pl.BlockSpec((rows, 2 * LANES), lambda i: (0, pair)),
        ]
        + ([whole(before), ANY] if pair else [ANY]),
        out_specs=[whole(s) for s in outs],
        scratch_shapes=[
            pltpu.VMEM((2, rows, LANES), F32),
            pltpu.VMEM((2, rows, LANES), F32),
            pltpu.VMEM((2, LANES, GROUP), BF),
            pltpu.VMEM((2, GROUP, LANES), BF),
            pltpu.VMEM((2, rows, LANES), BF),
            pltpu.VMEM((2, block, GROUP), F32),
        ],
        compiler_params=PARAMS,
        cost_estimate=cost(8 * 10**9, 4 * 10**6),
    )(offsets, q, own, theirs, *extra)


def pair_columns(pair):
    return (
        slice(pair * LANES, (pair + 1) * LANES),
        slice(2 * pair * LANES, (2 * pair + 1) * LANES),
        slice((2 * pair + 1) * LANES, (2 * pair + 2) * LANES),
    )


def blend(old, old_peak, more, more_peak):
    top = jnp.maximum(old_peak, more_peak)
    return old * jnp.exp2(old_peak - top) + more * jnp.exp2(more_peak - top), top


def middle_kernel(q, *refs, count):
    pieces, near_acc, near_peak = refs[:count], refs[count : count + 2], refs[count + 2 : count + 4]
    acc_out, peak_out, keys, values, slots = refs[count + 4 :]
    rows = q.shape[0]
    jobs = []
    for pair in range(2):
        lanes, k_at, v_at = pair_columns(pair)
        at = 0
        for piece in pieces:
            fill(keys.at[pair], values.at[pair], at, piece[:, k_at], piece[:, v_at])
            at += piece.shape[0]
        for head in range(2):

            def done(acc, peak, pair=pair, head=head):
                new, top = blend(near_acc[pair][head], near_peak[pair][head], acc, peak)
                acc_out[2 * pair + head] = new
                peak_out[2 * pair + head] = top

            jobs.append(
                (
                    lambda lanes=lanes, head=head: split_queries(q[:, lanes], head),
                    keys[pair, head],
                    values[pair, head],
                    done,
                    rows,
                )
            )
    attend(jobs, slots)


def middle_attention(q, pieces, near_acc, near_peak):
    rows, own = q.shape
    heads = own // HEAD_DIM
    return pl.pallas_call(
        functools.partial(middle_kernel, count=len(pieces)),
        out_shape=[shape(heads, rows, LANES, dtype=F32)] * 2,
        in_specs=[VMEM] * (5 + len(pieces)),
        out_specs=[VMEM] * 2,
        scratch_shapes=[
            pltpu.VMEM((2, 2, LANES, GROUP), BF),
            pltpu.VMEM((2, 2, GROUP, LANES), BF),
            pltpu.VMEM((2, rows, GROUP), F32),
        ],
        compiler_params=PARAMS,
        cost_estimate=cost(4 * 10**9, 4 * 10**6),
    )(q, *pieces, *near_acc, *near_peak)


def far_kernel(offsets, qf, *refs, count):
    pieces, (near_acc, near_peak) = refs[:count], (refs[count : count + 2], refs[count + 2 : count + 4])
    mid_acc, mid_peak, out, keys, values, slots, acc, peak, far_rows = refs[count + 4 :]
    mid, few = mid_acc.shape[1], qf.shape[0]
    acc[...] = mid_acc[...]
    peak[...] = mid_peak[...]
    jobs = []
    for pair in range(2):
        lanes, k_at, v_at = pair_columns(pair)
        at = 0
        for piece in pieces:
            fill(keys.at[pair], values.at[pair], at, piece[:, k_at], piece[:, v_at])
            at += piece.shape[0]
        for head in range(2):

            def done(more, more_peak, pair=pair, head=head):
                index = 2 * pair + head
                o_mid, o_far = offset_of(offsets, index, 0), offset_of(offsets, index, 1)
                shared = lax.rem(o_far, MID_RATE) == o_mid
                chosen = pl.ds(
                    lax.div(o_far, MID_RATE), few, stride=FAR_RATE // MID_RATE
                )
                held, held_peak = acc.at[index][chosen, :], peak.at[index][chosen, :]
                old = jnp.where(shared, held, near_acc[pair][head])
                old_peak = jnp.where(shared, held_peak, near_peak[pair][head])
                new, top = blend(old, old_peak, more, more_peak)
                acc.at[index][chosen, :] = jnp.where(shared, new, held)
                far_rows[index] = new

            jobs.append(
                (
                    lambda lanes=lanes, head=head: split_queries(qf[:, lanes], head),
                    keys[pair, head],
                    values[pair, head],
                    done,
                    few,
                )
            )
    attend(jobs, slots)
    for pair in range(2):
        lanes = pair_columns(pair)[0]
        out[:mid, lanes] = normalised(acc[2 * pair], acc[2 * pair + 1])
        out[mid:, lanes] = normalised(far_rows[2 * pair], far_rows[2 * pair + 1])


def far_attention(offsets, qf, pieces, near_acc, near_peak, mid_acc, mid_peak):
    few, own = qf.shape
    heads, mid = mid_acc.shape[:2]
    return pl.pallas_call(
        functools.partial(far_kernel, count=len(pieces)),
        out_shape=shape(mid + few, own),
        in_specs=[VMEM] * (8 + len(pieces)),
        out_specs=VMEM,
        scratch_shapes=[
            pltpu.VMEM((2, 2, LANES, GROUP), BF),
            pltpu.VMEM((2, 2, GROUP, LANES), BF),
            pltpu.VMEM((2, few, GROUP), F32),
            pltpu.VMEM((heads, mid, LANES), F32),
            pltpu.VMEM((heads, mid, LANES), F32),
            pltpu.VMEM((heads, few, LANES), F32),
        ],
        compiler_params=PARAMS,
        cost_estimate=cost(2 * 10**9, 4 * 10**6),
    )(offsets, qf, *pieces, *near_acc, *near_peak, mid_acc, mid_peak)


def out_kernel(me, *refs):
    early, late, weight, out, rows32 = refs[:4], refs[4:8], refs[8], refs[9], refs[10]
    rows, own = out.shape
    left = left_lanes()
    mid = rows // MID_RATE
    for d in range(4):
        for pair in range(2):
            rows32[2 * d + pair] = early[d][:rows, pair * LANES : (pair + 1) * LANES].astype(F32)
        told = early[d][rows:, :].astype(F32)
        for pair in range(2):
            lanes = slice(pair * LANES, (pair + 1) * LANES)
            target = rows32.at[2 * d + pair]
            for which, at, rate in ((0, slice(0, mid), MID_RATE), (1, slice(mid, None), FAR_RATE)):
                new = late[d][at, lanes].astype(F32)
                for head in range(2):
                    index = 2 * (2 * pair + head) + which
                    o = jnp.max(told[index : index + 1, :]).astype(jnp.int32)
                    chosen = pl.ds(o, rows // rate, stride=rate)
                    old = target[chosen, :]
                    target[chosen, :] = jnp.where(left, new, old) if head == 0 else jnp.where(left, old, new)
    block = 256
    for r in range(rows // block):
        at = slice(r * block, (r + 1) * block)
        total = None
        for d in range(4):
            depth = pl.ds(pl.multiple_of((me[0] ^ d) * own, own), own)
            part = jnp.concatenate([rows32[2 * d, at, :], rows32[2 * d + 1, at, :]], axis=1).astype(BF)
            term = jnp.dot(part, weight[depth, :], preferred_element_type=F32)
            total = term if total is None else total + term
        out[at, :] = total.astype(BF)


def project_out(me, early, late, weight):
    width = weight.shape[0]
    own = late[0].shape[1]
    rows = late[0].shape[0] * FAR_RATE // (FAR_RATE // MID_RATE + 1)

    def whole(s):
        return pl.BlockSpec(s.shape, lambda i, me: (0,) * len(s.shape))

    return pl.pallas_call(
        out_kernel,
        out_shape=shape(rows, own),
        grid_spec=pltpu.PrefetchScalarGridSpec(
            num_scalar_prefetch=1,
            grid=(1,),
            in_specs=[whole(a) for a in (*early, *late)]
            + [pl.BlockSpec((width, own), lambda i, me: (0, me[0]))],
            out_specs=pl.BlockSpec((rows, own), lambda i, me: (0, 0)),
            scratch_shapes=[pltpu.VMEM((8, rows, LANES), F32)],
        ),
        compiler_params=PARAMS,
        cost_estimate=cost(10**9, 4 * 10**6),
    )(me, *early, *late, weight)


def seg_move(array, target):
    pairs = []
    for i in range(64):
        x, z, core = i // 16, i // 2 % 8, i % 2
        x, z, core = target(x, z, core)
        pairs.append((i, (x % 4 * 8 + z % 8) * 2 + core))
    return lax.ppermute(array, "seg", pairs)


def swap_core(array):
    return seg_move(array, lambda x, z, core: (x, z, 1 - core))


def near_z(array, distance):
    return seg_move(array, lambda x, z, core: (x, z ^ distance, core))


def in_line(array):
    return seg_move(
        array, lambda x, z, core: (x, z // 4 * 4 + (z + (1 if core == 0 else 3)) % 4, core)
    )


def both_ways(array, distance):
    return seg_move(array, lambda x, z, core: (x, z + (distance if core == 0 else -distance), core))


def along_x(array, distance):
    return seg_move(array, lambda x, z, core: (x ^ distance, z, core))


def swap_head(array, distance):
    return lax.ppermute(array, "head", [(i, i ^ distance) for i in range(4)])


def pass_kernel(*refs):
    del refs


def hold(arrays, after):
    count = len(arrays)
    return pl.pallas_call(
        pass_kernel,
        out_shape=[shape(*a.shape, dtype=a.dtype) for a in arrays],
        in_specs=[ANY] * (count + 1),
        out_specs=[ANY] * count,
        input_output_aliases={i: i for i in range(count)},
        compiler_params=PARAMS,
    )(*arrays, after)


def shards(tokens, norm_gain, qkv_weight, out_weight, offsets):
    me = lax.axis_index("head").astype(jnp.int32).reshape(1)
    q, kv, qm, kvm, qf, kvf = project(offsets, tokens, norm_gain, qkv_weight)
    few = kvf.shape[0]
    chip = jnp.concatenate([kvf, swap_core(kvf)], axis=0)
    other = swap_core(kv)
    kvm_other = swap_core(kvm)
    one, two = both_ways(chip, 1), both_ways(chip, 2)
    onward = jnp.concatenate([chip, one[:few]], axis=0)
    three = both_ways(onward, 3)
    kvm, kvm_other = hold([kvm, kvm_other], onward)
    middle_chip = jnp.concatenate([kvm, kvm_other], axis=0)
    beside, across = in_line(middle_chip), near_z(kvm, 2)
    early, *near0 = near_attention(offsets, q, 0, kv, other, middle_chip)
    line = jnp.concatenate([kvf, *hold([one, two, three], early)], axis=0)
    columns = [along_x(line, distance) for distance in (1, 2, 3)]
    early, *near1 = near_attention(offsets, q, 1, kv, other, line, early)
    beside, across, *columns = hold([beside, across, *columns], early)
    middles = [kvm, kvm_other, beside, across, swap_core(beside), swap_core(across)]
    fars = [line, *columns]
    fars = fars + [swap_core(piece) for piece in fars]
    mid_acc, mid_peak = middle_attention(qm, middles, (near0[0], near1[0]), (near0[1], near1[1]))
    late = far_attention(
        offsets, qf, fars, (near0[2], near1[2]), (near0[3], near1[3]), mid_acc, mid_peak
    )
    earlies = [early] + [swap_head(early, d) for d in (1, 2, 3)]
    lates = [late] + [swap_head(late, d) for d in (1, 2, 3)]
    return project_out(me, earlies, lates, out_weight)


def solution(mesh):
    placed = (P("seg", None), P(), P(None, None, "head"), P(), P("head", None))
    return jax.shard_map(
        shards, mesh=mesh, in_specs=placed, out_specs=P("seg", "head"), check_vma=False
    )
```

time: 105 us -> 103 us (0.981)
  local copies, waits for them, and re-layouts: 6.22 us -> 14 us
  Pallas kernels: 42.1 us -> 35.1 us
  waiting for transfers between devices: 23.2 us -> 21.4 us
  starting transfers between devices: 33.1 us -> 31.4 us
    pallas_call x9 -> x5, Pallas kernels: 36.9 us -> 29.9 us  [the longest x2 15.3 us: near_attention(): pl.pallas_call(functools.partial(near_kernel, pair=pair), grid=(1,), out_...]
    unnamed x57 -> x55, local copies, waits for them, and re-layouts: 6.22 us -> 11.5 us
    ppermute x20 -> x17, starting transfers between devices: 25.3 us -> 22.5 us  [seg_move(): return lax.ppermute(array, 'seg', pairs)]
    concatenate x0 -> x3, local copies, waits for them, and re-layouts: none -> 2.51 us  [the longest x1 1.53 us: shards(): line = jnp.concatenate([kvf, *hold([one, two, three], early)], axis=0)]
    ppermute x20 -> x17, waiting for transfers between devices: 8.27 us -> 6.74 us  [seg_move(): return lax.ppermute(array, 'seg', pairs)]
  transfers between devices with their start and end apart: 26 -> 23, of which waited for: 9 -> 9; matrix products, arithmetic and copies ran while one was open for 0% -> 8% of each run, Pallas kernels for 24% -> 25%
where the time goes in v3:
time: 103 us
  Pallas kernels  35.1 us (34%)
  starting transfers between devices  31.4 us (30%)
  waiting for transfers between devices  21.4 us (21%)
  local copies, waits for them, and re-layouts  14 us (14%)
    ppermute x17, starting transfers between devices, seg_move(): return lax.ppermute(array, 'seg', pairs)  22.5 us
    pallas_call x2, Pallas kernels, near_attention(): pl.pallas_call(functools.partial(near_kernel, pair=pair), grid=(1,), out_...  15.3 us
    ppermute x6, waiting for transfers between devices, swap_head(): return lax.ppermute(array, 'head', [(i, i ^ distance) for i in range(4)])  14.7 us
    unnamed x55, local copies, waits for them, and re-layouts  11.5 us
    ppermute x6, starting transfers between devices, swap_head(): return lax.ppermute(array, 'head', [(i, i ^ distance) for i in range(4)])  8.84 us
    ppermute x17, waiting for transfers between devices, seg_move(): return lax.ppermute(array, 'seg', pairs)  6.74 us
    pallas_call x1, Pallas kernels, middle_attention(): pl.pallas_call(functools.partial(middle_kernel, count=len(pieces)), out_s...  5.92 us
    pallas_call x1, Pallas kernels, project(): pl.pallas_call(project_kernel, grid=(rows // block,), out_shape=[shape(ro...  5.18 us
  transfers between devices with their start and end apart: 23, of which 9 were waited for; matrix products, arithmetic and copies ran while one was open for 8% of the time, Pallas kernels for 25%

profile of v3, /device:TPU:1, one launch (start us, length us, event | category | flops | bytes accessed | tf_op | source)
XLA Modules:
  0.0 102.9 jit_solution(6527347535829097557)
XLA Ops:
  1.3 5.2 %shard_map.55 = (bf16[1024,256]{1,0:T(8,128)(2,1)}, bf16[1024,512]{1,0:T(8,128)(2,1)}, bf16[256,256]{1,0:T(8,128)(2,1)}, bf16[256,512]{1,0:T(8,128)(2,1)}, bf16[...) custom-call(s32[4,2]{1,0:T(4,128)} %copy.18.offsets, bf16[1024,1024]{1,0:T(8,128)(2,1)} %tokens.1, bf16[1024]{0:T(1024)(128)(2,1)} %gain.1, ...), custom_call_target="tpu_custom_call" | custom-call | flops 2000000000 | bytes 6000000 | tf_op jit(solution)/shard_map/pallas_call | solution.py:84
  6.5 3.3 %collective-permute-start = (bf16[1024,512]{1,0:T(8,128)(2,1)}, bf16[1024,512]{1,0:T(8,128)(2,1)S(1)}, u32[]{:S(2)}, u32[]{:S(2)}) collective-permute-start(bf16[1024,512]{1,0:T(8,128)(2,1)} %get-tuple-element.34.own), channel_id=1, source_target_pairs={{0,4},{4,0},{8,12},{12,8},{16,20},{20,16},{24,28},{28,24},{32,36},... | collective-permute-start | bytes 3145736 | tf_op jit(solution)/shard_map/ppermute | solution.py:432
  10.4 1.4 %constant_dynamic-update-slice_fusion.7 = (bf16[256,512]{1,0:T(8,128)(2,1)}, bf16[64,512]{1,0:T(8,128)(2,1)S(1)}) fusion(bf16[32,512]{1,0:T(8,128)(2,1)} %get-tuple-element.36), kind=kLoop, calls=%fused_computation.8 | loop fusion | bytes 98304
  12.4 3.8 %collective-permute-start.3 = (bf16[64,512]{1,0:T(8,128)(2,1)S(1)}, bf16[64,512]{1,0:T(8,128)(2,1)S(1)}, u32[]{:S(2)}, u32[]{:S(2)}) collective-permute-start(bf16[64,512]{1,0:T(8,128)(2,1)S(1)} %constant_dynamic-update-slice_fusion), channel_id=1, source_target_pairs={{0,8},{4,60},{8,16},{12,4},{16,24},{20,12},{24,32},{28,20},{32,40}... | collective-permute-start | bytes 196616 | tf_op jit(solution)/shard_map/ppermute | solution.py:432
  18.4 2.8 %collective-permute-start.5 = (bf16[96,512]{1,0:T(8,128)(2,1)S(1)}, bf16[96,512]{1,0:T(8,128)(2,1)S(1)}, u32[]{:S(2)}, u32[]{:S(2)}) collective-permute-start(bf16[96,512]{1,0:T(8,128)(2,1)S(1)} %pad_maximum_fusion.refs_2_), channel_id=1, source_target_pairs={{0,24},{4,44},{8,32},{12,52},{16,40},{20,60},{24,48},{28,4},{32,56... | collective-permute-start | bytes 294920 | tf_op jit(solution)/shard_map/ppermute | solution.py:432
  21.8 2.4 %collective-permute-start.10 = (bf16[256,512]{1,0:T(8,128)(2,1)}, bf16[256,512]{1,0:T(8,128)(2,1)S(1)}, u32[]{:S(2)}, u32[]{:S(2)}) collective-permute-start(bf16[256,512]{1,0:T(8,128)(2,1)} %get-tuple-element.37.refs_0_), channel_id=1, source_target_pairs={{0,16},{4,20},{8,24},{12,28},{16,0},{20,4},{24,8},{28,12},{32,48},... | collective-permute-start | bytes 786440 | tf_op jit(solution)/shard_map/ppermute | solution.py:432
  27.9 7.6 %shard_map.57 = (bf16[1024,128]{1,0:T(8,128)(2,1)}, f32[2,256,128]{2,1,0:T(8,128)}, f32[2,256,128]{2,1,0:T(8,128)}, f32[2,32,128]{2,1,0:T(8,128)}, f32[2,32,128]{2,1,0:T(8,128)}) custom-call(s32[4,2]{1,0:T(4,128)} %copy.18.offsets, bf16[1024,256]{1,0:T(8,128)(2,1)} %get-tuple-element.33.q, bf16[1024,512]{1,0:T(8,128)(2,1)} %get-tuple-element.34.own, ...), custom_call_target="tpu_custom_call" | custom-call | flops 8000000000 | bytes 4000000 | tf_op jit(solution)/shard_map/pallas_call | solution.py:218
  36.1 1.5 %constant_dynamic-update-slice_fusion.6 = bf16[256,512]{1,0:T(8,128)(2,1)} fusion(bf16[256,512]{1,0:T(8,128)(2,1)} %get-tuple-element.61, bf16[64,512]{1,0:T(8,128)(2,1)} %get-tuple-element.40), kind=kLoop, calls=%fused_computation.7 | loop fusion | bytes 131072
  37.6 1.5 %constant_dynamic-update-slice_fusion.5 = bf16[256,512]{1,0:T(8,128)(2,1)} fusion(bf16[256,512]{1,0:T(8,128)(2,1)} %constant_dynamic-update-slice_fusion.6, bf16[64,512]{1,0:T(8,128)(2,1)} %get-tuple-element.41), kind=kLoop, calls=%fused_computation.6 | loop fusion | bytes 131072
  39.1 1.5 %constant_dynamic-update-slice_fusion.4.refs_1_.refs_0_ = bf16[256,512]{1,0:T(8,128)(2,1)} fusion(bf16[256,512]{1,0:T(8,128)(2,1)} %constant_dynamic-update-slice_fusion.5, bf16[96,512]{1,0:T(8,128)(2,1)} %get-tuple-element.42), kind=kLoop, calls=%fused_computation.5 | loop fusion | bytes 196608 | tf_op jit(solution)/shard_map/concatenate | solution.py:491
  41.8 2.5 %collective-permute-start.12 = (bf16[256,512]{1,0:T(8,128)(2,1)}, bf16[256,512]{1,0:T(8,128)(2,1)S(1)}, u32[]{:S(2)}, u32[]{:S(2)}) collective-permute-start(bf16[256,512]{1,0:T(8,128)(2,1)} %constant_dynamic-update-slice_fusion.4.refs_1_.refs_0_), channel_id=1, source_target_pairs={{0,128},{4,132},{8,136},{12,140},{16,144},{20,148},{24,152},{28,15... | collective-permute-start | bytes 786440 | tf_op jit(solution)/shard_map/ppermute | solution.py:432
  44.4 7.8 %shard_map.59 = (bf16[1040,256]{1,0:T(8,128)(2,1)}, f32[2,256,128]{2,1,0:T(8,128)}, f32[2,256,128]{2,1,0:T(8,128)}, f32[2,32,128]{2,1,0:T(8,128)}, f32[2,32,128]{2,1,0:T(8,128)}) custom-call(s32[4,2]{1,0:T(4,128)} %copy.18.offsets, bf16[1024,256]{1,0:T(8,128)(2,1)} %get-tuple-element.33.q, bf16[1024,512]{1,0:T(8,128)(2,1)} %get-tuple-element.34.own, ...), custom_call_target="tpu_custom_call" | custom-call | flops 8000000000 | bytes 4000000 | tf_op jit(solution)/shard_map/pallas_call | solution.py:218
  52.3 1.5 %collective-permute-done.12.refs_3_ = bf16[256,512]{1,0:T(8,128)(2,1)S(1)} collective-permute-done((bf16[256,512]{1,0:T(8,128)(2,1)}, bf16[256,512]{1,0:T(8,128)(2,1)S(1)}, u32[]{:S(2)}, u32[]{:S(2)}) %collective-permute-start.12) | collective-permute-done | bytes 262176 | tf_op jit(solution)/shard_map/ppermute | solution.py:432
  53.8 4.1 %collective-permute-done.13.refs_4_ = bf16[256,512]{1,0:T(8,128)(2,1)S(1)} collective-permute-done((bf16[256,512]{1,0:T(8,128)(2,1)}, bf16[256,512]{1,0:T(8,128)(2,1)S(1)}, u32[]{:S(2)}, u32[]{:S(2)}) %collective-permute-start.13) | collective-permute-done | bytes 262176 | tf_op jit(solution)/shard_map/ppermute | solution.py:432
  58.5 2.2 %collective-permute-start.18 = (bf16[512,512]{1,0:T(8,128)(2,1)}, bf16[512,512]{1,0:T(8,128)(2,1)S(1)}, u32[]{:S(2)}, u32[]{:S(2)}) collective-permute-start(bf16[512,512]{1,0:T(8,128)(2,1)} %get-tuple-element.53.refs_2_), channel_id=1, source_target_pairs={{0,4},{4,0},{8,12},{12,8},{16,20},{20,16},{24,28},{28,24},{32,36},... | collective-permute-start | bytes 1572872 | tf_op jit(solution)/shard_map/ppermute | solution.py:432
  62.8 2.9 %collective-permute-start.7 = (bf16[1040,256]{1,0:T(8,128)(2,1)S(1)}, bf16[1040,256]{1,0:T(8,128)(2,1)S(1)}, u32[]{:S(2)}, u32[]{:S(2)}) collective-permute-start(bf16[1040,256]{1,0:T(8,128)(2,1)S(1)} %copy-done), channel_id=1, source_target_pairs={{0,2},{1,3},{2,0},{3,1},{4,6},{5,7},{6,4},{7,5},{8,10},{9,11},{10,... | collective-permute-start | bytes 1597448 | tf_op jit(solution)/shard_map/ppermute | solution.py:458
  68.3 5.9 %shard_map.61 = (f32[4,256,128]{2,1,0:T(8,128)}, f32[4,256,128]{2,1,0:T(8,128)}) custom-call(bf16[256,256]{1,0:T(8,128)(2,1)} %get-tuple-element.52.q, bf16[256,512]{1,0:T(8,128)(2,1)} %get-tuple-element.37.refs_0_, bf16[256,512]{1,0:T(8,128)(2,1)} %get-tuple-element.38.refs_1_, bf16[512,512]{1,0:T(8,128)(2,1)} %get-tuple-element.53.refs_2_, ...), custom_call_target="tpu_custom_call" | custom-call | flops 4000000000 | bytes 4000000 | tf_op jit(solution)/shard_map/pallas_call | solution.py:289
  75.0 4.1 %shard_map.62.refs_4_ = bf16[288,256]{1,0:T(8,128)(2,1)} custom-call(s32[4,2]{1,0:T(4,128)} %copy.18.offsets, bf16[32,256]{1,0:T(8,128)(2,1)} %get-tuple-element.44.qf, bf16[256,512]{1,0:T(8,128)(2,1)} %constant_dynamic-update-slice_fusion.4.refs_1_.refs_0_, bf16[256,512]{1,0:T(8,128)(2,1)} %get-tuple-element.45.refs_1_, ...), custom_call_target="tpu_custom_call" | custom-call | flops 2000000000 | bytes 4000000 | tf_op jit(solution)/shard_map/pallas_call | solution.py:352
  79.2 3.1 %collective-permute-start.21 = (bf16[288,256]{1,0:T(8,128)(2,1)}, bf16[288,256]{1,0:T(8,128)(2,1)S(1)}, u32[]{:S(2)}, u32[]{:S(2)}) collective-permute-start(bf16[288,256]{1,0:T(8,128)(2,1)} %shard_map.62.refs_4_), channel_id=1, source_target_pairs={{0,2},{1,3},{2,0},{3,1},{4,6},{5,7},{6,4},{7,5},{8,10},{9,11},{10,... | collective-permute-start | bytes 442376 | tf_op jit(solution)/shard_map/ppermute | solution.py:458
  83.0 5.3 %collective-permute-done.7.refs_2_ = bf16[1040,256]{1,0:T(8,128)(2,1)S(1)} collective-permute-done((bf16[1040,256]{1,0:T(8,128)(2,1)S(1)}, bf16[1040,256]{1,0:T(8,128)(2,1)S(1)}, u32[]{:S(2)}, u32[]{:S(2)}) %collective-permute-start.7) | collective-permute-done | bytes 532512 | tf_op jit(solution)/shard_map/ppermute | solution.py:458
  88.3 3.1 %collective-permute-done.8.refs_3_ = bf16[1040,256]{1,0:T(8,128)(2,1)S(1)} collective-permute-done((bf16[1040,256]{1,0:T(8,128)(2,1)S(1)}, bf16[1040,256]{1,0:T(8,128)(2,1)S(1)}, u32[]{:S(2)}, u32[]{:S(2)}) %collective-permute-start.8) | collective-permute-done | bytes 532512 | tf_op jit(solution)/shard_map/ppermute | solution.py:458
  91.4 3.3 %collective-permute-done.21.refs_6_ = bf16[288,256]{1,0:T(8,128)(2,1)S(1)} collective-permute-done((bf16[288,256]{1,0:T(8,128)(2,1)}, bf16[288,256]{1,0:T(8,128)(2,1)S(1)}, u32[]{:S(2)}, u32[]{:S(2)}) %collective-permute-start.21) | collective-permute-done | bytes 147488 | tf_op jit(solution)/shard_map/ppermute | solution.py:458
  94.7 3.0 %collective-permute-done.22.refs_7_ = bf16[288,256]{1,0:T(8,128)(2,1)S(1)} collective-permute-done((bf16[288,256]{1,0:T(8,128)(2,1)}, bf16[288,256]{1,0:T(8,128)(2,1)S(1)}, u32[]{:S(2)}, u32[]{:S(2)}) %collective-permute-start.22) | collective-permute-done | bytes 147488 | tf_op jit(solution)/shard_map/ppermute | solution.py:458
  98.3 4.5 %shard_map.63 = bf16[1024,256]{1,0:T(8,128)(2,1)} custom-call(s32[1]{0:T(128)} %bitcast.me, bf16[1040,256]{1,0:T(8,128)(2,1)} %get-tuple-element.43.refs_5_.refs_0_, bf16[1040,256]{1,0:T(8,128)(2,1)} %copy-done.2, bf16[1040,256]{1,0:T(8,128)(2,1)} %copy-done.3, bf16[1040,256]{1,0:T(8,128)(2,1)} %copy-done.4, bf16[288,256]{1,0:T(8,128)(2,1)} %shard_map.62.refs_4_, ...), custom_call_target="tpu_custom_call" | custom-call | flops 1000000000 | bytes 4000000 | tf_op jit(solution)/shard_map/pallas_call | solution.py:410
  (91 shorter events, 18.6 us)
Async XLA Ops:
  6.5 20.4 %collective-permute-start = (bf16[1024,512]{1,0:T(8,128)(2,1)}, bf16[1024,512]{1,0:T(8,128)(2,1)S(1)}, u32[]{:S(2)}, u32[]{:S(2)}) collective-permute-start(bf16[1024,512]{1,0:T(8,128)(2,1)} %get-tuple-element.34.own), channel_id=1, source_target_pairs={{0,4},{4,0},{8,12},{12,8},{16,20},{20,16},{24,28},{28,24},{32,36},... | collective-permute-start | bytes 3145736 | tf_op jit(solution)/shard_map/ppermute | solution.py:432
  9.8 2.5 %collective-permute-start.2 = (bf16[32,512]{1,0:T(8,128)(2,1)}, bf16[32,512]{1,0:T(8,128)(2,1)S(1)}, u32[]{:S(2)}, u32[]{:S(2)}) collective-permute-start(bf16[32,512]{1,0:T(8,128)(2,1)} %get-tuple-element.36), channel_id=1, source_target_pairs={{0,4},{4,0},{8,12},{12,8},{16,20},{20,16},{24,28},{28,24},{32,36},... | collective-permute-start | bytes 98312 | tf_op jit(solution)/shard_map/ppermute | solution.py:432
  9.9 11.2 %collective-permute-start.1 = (bf16[256,512]{1,0:T(8,128)(2,1)}, bf16[256,512]{1,0:T(8,128)(2,1)S(1)}, u32[]{:S(2)}, u32[]{:S(2)}) collective-permute-start(bf16[256,512]{1,0:T(8,128)(2,1)} %get-tuple-element.35.refs_0_), channel_id=1, source_target_pairs={{0,4},{4,0},{8,12},{12,8},{16,20},{20,16},{24,28},{28,24},{32,36},... | collective-permute-start | bytes 786440 | tf_op jit(solution)/shard_map/ppermute | solution.py:432
  12.4 5.2 %collective-permute-start.3 = (bf16[64,512]{1,0:T(8,128)(2,1)S(1)}, bf16[64,512]{1,0:T(8,128)(2,1)S(1)}, u32[]{:S(2)}, u32[]{:S(2)}) collective-permute-start(bf16[64,512]{1,0:T(8,128)(2,1)S(1)} %constant_dynamic-update-slice_fusion), channel_id=1, source_target_pairs={{0,8},{4,60},{8,16},{12,4},{16,24},{20,12},{24,32},{28,20},{32,40}... | collective-permute-start | bytes 196616 | tf_op jit(solution)/shard_map/ppermute | solution.py:432
  16.2 19.2 %collective-permute-start.4 = (bf16[64,512]{1,0:T(8,128)(2,1)S(1)}, bf16[64,512]{1,0:T(8,128)(2,1)S(1)}, u32[]{:S(2)}, u32[]{:S(2)}) collective-permute-start(bf16[64,512]{1,0:T(8,128)(2,1)S(1)} %constant_dynamic-update-slice_fusion), channel_id=1, source_target_pairs={{0,16},{4,52},{8,24},{12,60},{16,32},{20,4},{24,40},{28,12},{32,48... | collective-permute-start | bytes 196616 | tf_op jit(solution)/shard_map/ppermute | solution.py:432
  17.6 17.9 %copy-start.6 = (bf16[64,512]{1,0:T(8,128)(2,1)}, bf16[64,512]{1,0:T(8,128)(2,1)S(1)}, u32[]{:S(2)}) copy-start(bf16[64,512]{1,0:T(8,128)(2,1)S(1)} %collective-permute-done.3.refs_0_) | copy-start | bytes 196612
  18.4 17.1 %collective-permute-start.5 = (bf16[96,512]{1,0:T(8,128)(2,1)S(1)}, bf16[96,512]{1,0:T(8,128)(2,1)S(1)}, u32[]{:S(2)}, u32[]{:S(2)}) collective-permute-start(bf16[96,512]{1,0:T(8,128)(2,1)S(1)} %pad_maximum_fusion.refs_2_), channel_id=1, source_target_pairs={{0,24},{4,44},{8,32},{12,52},{16,40},{20,60},{24,48},{28,4},{32,56... | collective-permute-start | bytes 294920 | tf_op jit(solution)/shard_map/ppermute | solution.py:432
  21.8 30.4 %collective-permute-start.10 = (bf16[256,512]{1,0:T(8,128)(2,1)}, bf16[256,512]{1,0:T(8,128)(2,1)S(1)}, u32[]{:S(2)}, u32[]{:S(2)}) collective-permute-start(bf16[256,512]{1,0:T(8,128)(2,1)} %get-tuple-element.37.refs_0_), channel_id=1, source_target_pairs={{0,16},{4,20},{8,24},{12,28},{16,0},{20,4},{24,8},{28,12},{32,48},... | collective-permute-start | bytes 786440 | tf_op jit(solution)/shard_map/ppermute | solution.py:432
  26.2 26.0 %collective-permute-start.9 = (bf16[512,512]{1,0:T(8,128)(2,1)S(1)}, bf16[512,512]{1,0:T(8,128)(2,1)S(1)}, u32[]{:S(2)}, u32[]{:S(2)}) collective-permute-start(bf16[512,512]{1,0:T(8,128)(2,1)S(1)} %constant_dynamic-update-slice_fusion.2.refs_0_), channel_id=1, source_target_pairs={{0,8},{4,28},{8,16},{12,4},{16,24},{20,12},{24,0},{28,20},{32,40},... | collective-permute-start | bytes 1572872 | tf_op jit(solution)/shard_map/ppermute | solution.py:432
  40.6 11.7 %collective-permute-start.11 = (bf16[256,512]{1,0:T(8,128)(2,1)}, bf16[256,512]{1,0:T(8,128)(2,1)S(1)}, u32[]{:S(2)}, u32[]{:S(2)}) collective-permute-start(bf16[256,512]{1,0:T(8,128)(2,1)} %constant_dynamic-update-slice_fusion.4.refs_1_.refs_0_), channel_id=1, source_target_pairs={{0,64},{4,68},{8,72},{12,76},{16,80},{20,84},{24,88},{28,92},{32,9... | collective-permute-start | bytes 786440 | tf_op jit(solution)/shard_map/ppermute | solution.py:432
  41.8 12.0 %collective-permute-start.12 = (bf16[256,512]{1,0:T(8,128)(2,1)}, bf16[256,512]{1,0:T(8,128)(2,1)S(1)}, u32[]{:S(2)}, u32[]{:S(2)}) collective-permute-start(bf16[256,512]{1,0:T(8,128)(2,1)} %constant_dynamic-update-slice_fusion.4.refs_1_.refs_0_), channel_id=1, source_target_pairs={{0,128},{4,132},{8,136},{12,140},{16,144},{20,148},{24,152},{28,15... | collective-permute-start | bytes 786440 | tf_op jit(solution)/shard_map/ppermute | solution.py:432
  44.3 13.6 %collective-permute-start.13 = (bf16[256,512]{1,0:T(8,128)(2,1)}, bf16[256,512]{1,0:T(8,128)(2,1)S(1)}, u32[]{:S(2)}, u32[]{:S(2)}) collective-permute-start(bf16[256,512]{1,0:T(8,128)(2,1)} %constant_dynamic-update-slice_fusion.4.refs_1_.refs_0_), channel_id=1, source_target_pairs={{0,192},{4,196},{8,200},{12,204},{16,208},{20,212},{24,216},{28,22... | collective-permute-start | bytes 786440 | tf_op jit(solution)/shard_map/ppermute | solution.py:432
  58.5 8.9 %collective-permute-start.18 = (bf16[512,512]{1,0:T(8,128)(2,1)}, bf16[512,512]{1,0:T(8,128)(2,1)S(1)}, u32[]{:S(2)}, u32[]{:S(2)}) collective-permute-start(bf16[512,512]{1,0:T(8,128)(2,1)} %get-tuple-element.53.refs_2_), channel_id=1, source_target_pairs={{0,4},{4,0},{8,12},{12,8},{16,20},{20,16},{24,28},{28,24},{32,36},... | collective-permute-start | bytes 1572872 | tf_op jit(solution)/shard_map/ppermute | solution.py:432
  60.7 2.1 %collective-permute-start.14 = (bf16[256,512]{1,0:T(8,128)(2,1)}, bf16[256,512]{1,0:T(8,128)(2,1)S(1)}, u32[]{:S(2)}, u32[]{:S(2)}) collective-permute-start(bf16[256,512]{1,0:T(8,128)(2,1)} %constant_dynamic-update-slice_fusion.4.refs_1_.refs_0_), channel_id=1, source_target_pairs={{0,4},{4,0},{8,12},{12,8},{16,20},{20,16},{24,28},{28,24},{32,36},... | collective-permute-start | bytes 786440 | tf_op jit(solution)/shard_map/ppermute | solution.py:432
  60.7 5.0 %collective-permute-start.19 = (bf16[256,512]{1,0:T(8,128)(2,1)}, bf16[256,512]{1,0:T(8,128)(2,1)S(1)}, u32[]{:S(2)}, u32[]{:S(2)}) collective-permute-start(bf16[256,512]{1,0:T(8,128)(2,1)} %get-tuple-element.54.refs_3_), channel_id=1, source_target_pairs={{0,4},{4,0},{8,12},{12,8},{16,20},{20,16},{24,28},{28,24},{32,36},... | collective-permute-start | bytes 786440 | tf_op jit(solution)/shard_map/ppermute | solution.py:432
  61.2 5.3 %collective-permute-start.15 = (bf16[256,512]{1,0:T(8,128)(2,1)}, bf16[256,512]{1,0:T(8,128)(2,1)S(1)}, u32[]{:S(2)}, u32[]{:S(2)}) collective-permute-start(bf16[256,512]{1,0:T(8,128)(2,1)} %get-tuple-element.45.refs_1_), channel_id=1, source_target_pairs={{0,4},{4,0},{8,12},{12,8},{16,20},{20,16},{24,28},{28,24},{32,36},... | collective-permute-start | bytes 786440 | tf_op jit(solution)/shard_map/ppermute | solution.py:432
  61.2 21.0 %collective-permute-start.6 = (bf16[1040,256]{1,0:T(8,128)(2,1)S(1)}, bf16[1040,256]{1,0:T(8,128)(2,1)S(1)}, u32[]{:S(2)}, u32[]{:S(2)}) collective-permute-start(bf16[1040,256]{1,0:T(8,128)(2,1)S(1)} %copy-done), channel_id=1, source_target_pairs={{0,1},{1,0},{2,3},{3,2},{4,5},{5,4},{6,7},{7,6},{8,9},{9,8},{10,11... | collective-permute-start | bytes 1597448 | tf_op jit(solution)/shard_map/ppermute | solution.py:458
  62.8 25.4 %collective-permute-start.7 = (bf16[1040,256]{1,0:T(8,128)(2,1)S(1)}, bf16[1040,256]{1,0:T(8,128)(2,1)S(1)}, u32[]{:S(2)}, u32[]{:S(2)}) collective-permute-start(bf16[1040,256]{1,0:T(8,128)(2,1)S(1)} %copy-done), channel_id=1, source_target_pairs={{0,2},{1,3},{2,0},{3,1},{4,6},{5,7},{6,4},{7,5},{8,10},{9,11},{10,... | collective-permute-start | bytes 1597448 | tf_op jit(solution)/shard_map/ppermute | solution.py:458
  65.8 25.6 %collective-permute-start.8 = (bf16[1040,256]{1,0:T(8,128)(2,1)S(1)}, bf16[1040,256]{1,0:T(8,128)(2,1)S(1)}, u32[]{:S(2)}, u32[]{:S(2)}) collective-permute-start(bf16[1040,256]{1,0:T(8,128)(2,1)S(1)} %copy-done), channel_id=1, source_target_pairs={{0,3},{1,2},{2,1},{3,0},{4,7},{5,6},{6,5},{7,4},{8,11},{9,10},{10,... | collective-permute-start | bytes 1597448 | tf_op jit(solution)/shard_map/ppermute | solution.py:458
  66.5 7.7 %collective-permute-start.16 = (bf16[256,512]{1,0:T(8,128)(2,1)}, bf16[256,512]{1,0:T(8,128)(2,1)S(1)}, u32[]{:S(2)}, u32[]{:S(2)}) collective-permute-start(bf16[256,512]{1,0:T(8,128)(2,1)} %get-tuple-element.46.refs_2_), channel_id=1, source_target_pairs={{0,4},{4,0},{8,12},{12,8},{16,20},{20,16},{24,28},{28,24},{32,36},... | collective-permute-start | bytes 786440 | tf_op jit(solution)/shard_map/ppermute | solution.py:432
  67.5 6.8 %collective-permute-start.17 = (bf16[256,512]{1,0:T(8,128)(2,1)}, bf16[256,512]{1,0:T(8,128)(2,1)S(1)}, u32[]{:S(2)}, u32[]{:S(2)}) collective-permute-start(bf16[256,512]{1,0:T(8,128)(2,1)} %get-tuple-element.47.refs_3_), channel_id=1, source_target_pairs={{0,4},{4,0},{8,12},{12,8},{16,20},{20,16},{24,28},{28,24},{32,36},... | collective-permute-start | bytes 786440 | tf_op jit(solution)/shard_map/ppermute | solution.py:432
  79.2 12.2 %collective-permute-start.20 = (bf16[288,256]{1,0:T(8,128)(2,1)}, bf16[288,256]{1,0:T(8,128)(2,1)S(1)}, u32[]{:S(2)}, u32[]{:S(2)}) collective-permute-start(bf16[288,256]{1,0:T(8,128)(2,1)} %shard_map.62.refs_4_), channel_id=1, source_target_pairs={{0,1},{1,0},{2,3},{3,2},{4,5},{5,4},{6,7},{7,6},{8,9},{9,8},{10,11... | collective-permute-start | bytes 442376 | tf_op jit(solution)/shard_map/ppermute | solution.py:458
  79.2 15.5 %collective-permute-start.21 = (bf16[288,256]{1,0:T(8,128)(2,1)}, bf16[288,256]{1,0:T(8,128)(2,1)S(1)}, u32[]{:S(2)}, u32[]{:S(2)}) collective-permute-start(bf16[288,256]{1,0:T(8,128)(2,1)} %shard_map.62.refs_4_), channel_id=1, source_target_pairs={{0,2},{1,3},{2,0},{3,1},{4,6},{5,7},{6,4},{7,5},{8,10},{9,11},{10,... | collective-permute-start | bytes 442376 | tf_op jit(solution)/shard_map/ppermute | solution.py:458
  82.3 15.4 %collective-permute-start.22 = (bf16[288,256]{1,0:T(8,128)(2,1)}, bf16[288,256]{1,0:T(8,128)(2,1)S(1)}, u32[]{:S(2)}, u32[]{:S(2)}) collective-permute-start(bf16[288,256]{1,0:T(8,128)(2,1)} %shard_map.62.refs_4_), channel_id=1, source_target_pairs={{0,3},{1,2},{2,1},{3,0},{4,7},{5,6},{6,5},{7,4},{8,11},{9,10},{10,... | collective-permute-start | bytes 442376 | tf_op jit(solution)/shard_map/ppermute | solution.py:458
  (24 other events, 101.8 us)
